TPU v7x, 128 devices: a whole 4x4x4 slice. The times are simulated.
128 devices in a mesh: phi: 8 (over z, core), theta: 8 (over x, y_hi), row: 2 (over y_lo).
Axes of the slice: x: 4, y: 4 (y_hi: 2, y_lo: 2; y = y_hi * 2 + y_lo), z: 4, core: 2. Of those that a mesh axis runs over, the one named last changes fastest.
Arguments:
- test_fields: float32 [27, 8, 256, 2048], P(None, 'row', 'theta', 'phi'), may hold values from -6 to 6
- velocity: float32 [3, 8, 256, 2048], P(None, 'row', 'theta', 'phi'), may hold values from -6 to 6
- kept: int32 [256], P('theta'), may hold values from 64 to 512, as said below
Outputs:
- result: float32 [27, 8, 256, 2048], P(None, 'row', 'theta', 'phi')
- emf: float32 [27, 8, 256], P(None, 'row', ('theta', 'phi'))
Inputs may be any that keep to these rules, and one draw needn't show every extreme that they name: `kept`: row 0 keeps 512 modes.
All inputs are finite; a program needn't handle non-finite values.
Results may differ from a plain program's by a relative error of at most 0.000094.
Values sent between devices are 32-bit elements; how exact they have to be, the bound alone decides.
A program may use at most 128 MiB of HBM per device.

v0:
```python
import math

import jax
import jax.numpy as jnp
from jax import lax
from jax.sharding import PartitionSpec as P

NPHI = 2048
MMAX = 512


inner_radius = 0.7
shell_depth = 0.3
coef_radial = 0.2
coef_polar = 0.1
source_step = 0.5


def with_halo(x, sides, width):
    for axis, dim in sides:
        devices, length = (lax.axis_size(axis), x.shape[dim])
        up = [(i, (i + 1) % devices) for i in range(devices - 1)]
        down = [(j, i) for i, j in up]
        last = lax.slice_in_dim(x, length - width, length, axis=dim)
        initial = lax.slice_in_dim(x, 0, width, axis=dim)
        before = lax.ppermute(last, axis, up)
        after = lax.ppermute(initial, axis, down)
        x = jnp.concatenate([before, x, after], axis=dim)
    return x


def fourier_tables(first_cell, cell_total):
    mode_index = jnp.arange(MMAX, dtype=jnp.int32)[:, None]
    cell_index = (first_cell + jnp.arange(cell_total, dtype=jnp.int32))[None, :]
    angles = (mode_index * cell_index % NPHI).astype(jnp.float32) * jnp.float32(
        2.0 * math.pi / NPHI
    )
    return (jnp.cos(angles), jnp.sin(angles))


def mode_weights(counts):
    mode_index = jnp.arange(MMAX, dtype=jnp.int32)[None, :]
    mode_scale = jnp.where(mode_index == 0, jnp.float32(1.0 / NPHI), jnp.float32(2.0 / NPHI))
    return jnp.where(mode_index < counts[:, None], mode_scale, jnp.float32(0.0))


def geometry(radial_index, polar_index, radial_total, polar_total):
    cell_width = shell_depth / radial_total
    radius = inner_radius + cell_width * (radial_index.astype(jnp.float32) + 0.5)
    outward = ((radius + 0.5 * cell_width) / radius) ** 2
    inward = ((radius - 0.5 * cell_width) / radius) ** 2
    metric = (1.0 / radius) ** 2
    angle_step = math.pi / polar_total
    polar_angle = angle_step * (polar_index.astype(jnp.float32) + 0.5)
    north_side = jnp.sin(polar_angle - 0.5 * angle_step) / jnp.sin(polar_angle)
    south_side = jnp.sin(polar_angle + 0.5 * angle_step) / jnp.sin(polar_angle)
    polar_rows = ((2 * polar_index + 1) * 3 < polar_total) | (
        (2 * (polar_total - 1 - polar_index) + 1) * 3 < polar_total
    )
    profiles = jnp.stack([jnp.ones_like(polar_angle), jnp.cos(polar_angle), jnp.sin(polar_angle)])
    return (outward, inward, metric, north_side, south_side, polar_rows, profiles)


def diffuse(padded, outward, inward, metric, north_side, south_side):
    center = padded[:, 1:-1, 1:-1]
    radial_part = outward[:, None, None] * (padded[:, 2:, 1:-1] - center) - inward[
        :, None, None
    ] * (center - padded[:, :-2, 1:-1])
    polar_part = south_side[None, :, None] * (padded[:, 1:-1, 2:] - center) - north_side[
        None, :, None
    ] * (center - padded[:, 1:-1, :-2])
    return coef_radial * radial_part + coef_polar * metric[:, None, None] * polar_part


def sources(velocity, profiles):
    vel_radial, vel_polar, vel_azimuth = (velocity[0], velocity[1], velocity[2])
    zero_part = jnp.zeros_like(vel_radial)
    crossed = jnp.stack(
        [
            jnp.stack([zero_part, vel_azimuth, -vel_polar]),
            jnp.stack([-vel_azimuth, zero_part, vel_radial]),
            jnp.stack([vel_polar, -vel_radial, zero_part]),
        ]
    )
    source = crossed[:, None] * profiles[None, :, None, None, :, None]
    return source.reshape((27,) + vel_radial.shape)


def emf_terms(velocity, field_data):
    grouped = field_data.reshape((9, 3) + field_data.shape[1:])
    first_term = velocity[1] * grouped[:, 2] - velocity[2] * grouped[:, 1]
    second_term = velocity[2] * grouped[:, 0] - velocity[0] * grouped[:, 2]
    third_term = velocity[0] * grouped[:, 1] - velocity[1] * grouped[:, 0]
    crossed = jnp.stack([first_term, second_term, third_term], axis=1)
    return jnp.sum(crossed, axis=-1).reshape((27,) + field_data.shape[1:3])


def body(test_fields, velocity, kept):
    components, cells_radial, cells_polar, cells_azimuth = test_fields.shape
    theta_devices = lax.axis_size("theta")
    polar_total = cells_polar * theta_devices
    radial_index = lax.axis_index("row") * cells_radial + jnp.arange(cells_radial, dtype=jnp.int32)
    polar_index = lax.axis_index("theta") * cells_polar + jnp.arange(cells_polar, dtype=jnp.int32)
    outward, inward, metric, north_side, south_side, polar_rows, profiles = geometry(
        radial_index, polar_index, cells_radial * lax.axis_size("row"), polar_total
    )
    padded = with_halo(test_fields, (("theta", 2), ("row", 1)), 1)
    stepped = (
        test_fields
        + diffuse(padded, outward, inward, metric, north_side, south_side)
        + source_step * sources(velocity, profiles)
    )
    field_lines = stepped.reshape(-1, cells_azimuth)
    counts = jnp.broadcast_to(kept[None, None, :], (components, cells_radial, cells_polar)).reshape(
        -1
    )
    polar_lines = jnp.broadcast_to(
        polar_rows[None, None, :], (components, cells_radial, cells_polar)
    ).reshape(-1)
    phi_index = lax.axis_index("phi")
    cos_table, sin_table = fourier_tables(phi_index * cells_azimuth, cells_azimuth)
    cosine_part = jnp.dot(field_lines, cos_table.T, precision=lax.Precision.HIGHEST)
    sine_part = jnp.dot(field_lines, sin_table.T, precision=lax.Precision.HIGHEST)
    cosine_part, sine_part = lax.psum((cosine_part, sine_part), "phi")
    weights = mode_weights(counts)
    smooth = jnp.dot(cosine_part * weights, cos_table, precision=lax.Precision.HIGHEST)
    smooth = smooth + jnp.dot(sine_part * weights, sin_table, precision=lax.Precision.HIGHEST)
    restored = jnp.where(polar_lines[:, None], smooth, field_lines)
    result = restored.reshape(stepped.shape)
    partial_sum = emf_terms(velocity, result) / NPHI
    emf = lax.psum_scatter(partial_sum, "phi", scatter_dimension=2, tiled=True)
    return (result, emf)


def solution(mesh):
    return jax.shard_map(
        body,
        mesh=mesh,
        in_specs=(P(None, "row", "theta", "phi"), P(None, "row", "theta", "phi"), P("theta")),
        out_specs=(P(None, "row", "theta", "phi"), P(None, "row", ("theta", "phi"))),
        check_vma=False,
    )
```

profile of v0, /device:TPU:1, one launch (start us, length us, event | category | flops | bytes accessed | tf_op | source)
XLA Modules:
  0.0 294.6 jit_solution(11823510628587535641)
XLA Ops:
  7.2 0.0 all-reduce.4.cloned.1.call-start
  7.2 1.6 fusion.63
  8.8 0.0 copy-start.6
  8.9 5.8 %collective-permute-start = (f32[27,4,1,256]{3,0,2,1:T(8,128)S(1)}, f32[27,4,1,256]{3,0,2,1:T(8,128)S(1)}, u32[]{:S(2)}, u32[]{:S(2)}) collective-permute-start(f32[27,4,1,256]{3,0,2,1:T(8,128)S(1)} %copy.14), channel_id=1, source_target_pairs={{0,2},{2,4},{4,6},{6,8},{8,10},{10,12},{12,14},{1,3},{3,5},{5,7},{... | collective-permute-start | bytes 331784 | tf_op jit(solution)/shard_map/ppermute | solution.py:26
  14.7 1.3 collective-permute-start.1
  16.1 0.1 pad_maximum_fusion.12
  16.2 0.6 collective-permute-done
  16.8 0.1 copy.8
  16.9 5.0 %collective-permute-done.1 = f32[27,4,1,256]{3,0,2,1:T(8,128)S(1)} collective-permute-done((f32[27,4,1,256]{3,0,2,1:T(8,128)S(1)}, f32[27,4,1,256]{3,0,2,1:T(8,128)S(1)}, u32[]{:S(2)}, u32[]{:S(2)}) %collective-permute-start.1) | collective-permute-done | bytes 110624 | tf_op jit(solution)/shard_map/ppermute | solution.py:27
  21.9 0.1 copy.9
  22.0 1.7 pad_maximum_fusion.11
  23.7 0.0 copy-start
  23.8 1.6 collective-permute-start.2
  25.3 4.1 %collective-permute-start.3 = (f32[27,1,34,256]{3,2,1,0:T(8,128)S(1)}, f32[27,1,34,256]{3,2,1,0:T(8,128)S(1)}, u32[]{:S(2)}, u32[]{:S(2)}) collective-permute-start(f32[27,1,34,256]{3,2,1,0:T(8,128)S(1)} %get-tuple-element.9), channel_id=1, source_target_pairs={{0,1},{2,3},{4,5},{6,7},{8,9},{10,11},{12,13},{14,15},{16,17},{18,... | collective-permute-start | bytes 2820104 | tf_op jit(solution)/shard_map/ppermute | solution.py:26
  29.5 0.1 sine_divide_fusion
  29.6 0.0 copy-done.6
  29.6 0.0 copy-start.8
  29.6 0.8 slice_bitcast_fusion.2
  30.4 0.1 maximum_bitcast_fusion
  30.6 0.1 pad_maximum_fusion.8
  30.7 19.0 %collective-permute-done.2 = f32[27,1,34,256]{3,2,1,0:T(8,128)S(1)} collective-permute-done((f32[27,1,34,256]{3,2,1,0:T(8,128)S(1)}, f32[27,1,34,256]{3,2,1,0:T(8,128)S(1)}, u32[]{:S(2)}, u32[]{:S(2)}) %collective-permute-start.2) | collective-permute-done | bytes 940064 | tf_op jit(solution)/shard_map/ppermute | solution.py:27
  49.7 1.0 collective-permute-done.3
  50.7 0.0 copy-done
  50.7 5.7 %fusion.10 = f32[27,4,32,256]{3,2,1,0:T(8,128)S(1)} fusion(f32[27,4,32,256]{3,2,1,0:T(8,128)S(1)} %copy-done, f32[27,4,1,256]{3,2,1,0:T(1,128)S(1)} %copy.8, f32[27,4,1,256]{3,2,1,0:T(1,128)S(1)} %copy.9, f32[27,1,34,256]{3,2,1,0:T(8,128)S(1)} %collective-permute-done.3, f32[27,1,34,256]{3,2,1,0:T(8,128)S(1)} %collective-permute-done.2, ...), kind=kLoop, calls=%fused_computation.14 | loop fusion | flops 22118400 | bytes 10362544 | tf_op jit(solution)/shard_map/add | solution.py:109
  56.4 11.7 %fusion.38 = f32[3456,512]{1,0:T(8,128)} fusion(f32[3456,256]{1,0:T(8,128)S(1)} %bitcast.26, s32[256]{0:T(256)S(1)} %iota_add_fusion), kind=kOutput, calls=%fused_computation.61 | convolution fusion | flops 5437652992 | bytes 10617856 | tf_op jit(solution)/shard_map/dot_general | solution.py:123
  68.1 0.0 copy-done.8
  68.1 11.5 %fusion.35 = f32[3456,512]{1,0:T(8,128)} fusion(f32[3456,256]{1,0:T(8,128)S(1)} %bitcast.27, s32[256]{0:T(256)S(1)} %iota_add_fusion), kind=kOutput, calls=%fused_computation.60 | convolution fusion | flops 5437652992 | bytes 10617856 | tf_op jit(solution)/shard_map/dot_general | solution.py:122
  79.6 0.0 all-reduce.4.cloned.1.call-update
  79.7 0.6 copy-done.11
  80.3 0.6 broadcast_in_dim.52
  80.9 0.9 lt.39
  81.8 0.6 broadcast_in_dim.49
  82.4 1.4 broadcast_in_dim.50
  83.8 1.2 dynamic-slice
  85.7 0.6 fusion.40
  86.3 156.8 %all-reduce.4.cloned.1.call-done = (f32[3456,512]{1,0:T(8,128)}, f32[3456,512]{1,0:T(8,128)}) async-done(((f32[3456,512]{1,0:T(8,128)}, f32[3456,512]{1,0:T(8,128)}), (f32[3456,512]{1,0:T(8,128)}, f32[3456,512]{1,0:T(8,128)})) %all-reduce.4.cloned.1.call-update) | async-done | bytes 14155792 | tf_op jit(solution)/shard_map/psum | solution.py:124
  243.1 11.3 %fusion = f32[3456,256]{1,0:T(8,128)S(1)} fusion(f32[3456,512]{1,0:T(8,128)} %get-tuple-element.6, f32[512]{0:T(512)} %fusion.40, s32[3456]{0:T(1024)S(1)} %lt.39, s32[256]{0:T(256)} %copy-done.8), kind=kOutput, calls=%fused_computation.2 | convolution fusion | flops 5442961408 | bytes 10633728 | tf_op jit(solution)/shard_map/dot_general | solution.py:126
  254.4 0.0 copy-done.2
  254.4 0.0 copy-done.7
  254.4 0.0 copy-done.9
  254.5 8.3 %fusion.3 = f32[3456,256]{1,0:T(8,128)S(1)} fusion(f32[3456,256]{1,0:T(8,128)S(1)} %bitcast.28, f32[3456,256]{1,0:T(8,128)S(1)} %fusion, f32[3456,512]{1,0:T(8,128)S(1)} %copy-done.2, f32[512]{0:T(512)S(1)} %copy-done.10, s32[3456]{0:T(1024)S(1)} %lt.39, pred[3456]{0:T(1024)(128)(4,1)S(1)} %copy-done.7, s32[256]{0:T(256)S(1)} %copy-done.9), kind=kOutput, calls=%fused_computation.6 | convolution fusion | flops 5444730880 | bytes 17715072 | tf_op jit(solution)/shard_map/dot_general | solution.py:127
  262.8 0.0 copy-start.1
  262.8 0.5 multiply_subtract_fusion.2
  263.4 1.2 copy-done.1
  264.6 0.6 maximum_reduce_fusion
  265.2 0.1 copy.12
  265.3 21.9 %all-reduce = f32[27,4,32]{0,1,2:T(4,128)S(1)} all-reduce(f32[27,4,32]{0,1,2:T(4,128)S(1)} %copy.12), channel_id=2, replica_groups=mesh['phi'=8,'theta'=8,'row'=2] {'phi'}, use_global_device_ids=true, to_apply=%region_3.4.clone | all-reduce | flops 3456 | bytes 27648
  287.2 0.6 copy.13
  (25 shorter events, 0.2 us)
Async XLA Ops:
  7.2 236.0 %all-reduce.4.cloned.1.call-start = ((), (), s32[]{:S(2)}) async-start(), calls=%async_computation | async-start | bytes 28311552 | tf_op jit(solution)/shard_map/psum | solution.py:124
  8.8 20.7 %copy-start.6 = (f32[3,4,32,256]{3,2,1,0:T(8,128)S(1)}, f32[3,4,32,256]{3,2,1,0:T(8,128)}, u32[]{:S(2)}) copy-start(f32[3,4,32,256]{3,2,1,0:T(8,128)} %param.4) | copy-start | bytes 1179652
  8.9 7.9 %collective-permute-start = (f32[27,4,1,256]{3,0,2,1:T(8,128)S(1)}, f32[27,4,1,256]{3,0,2,1:T(8,128)S(1)}, u32[]{:S(2)}, u32[]{:S(2)}) collective-permute-start(f32[27,4,1,256]{3,0,2,1:T(8,128)S(1)} %copy.14), channel_id=1, source_target_pairs={{0,2},{2,4},{4,6},{6,8},{8,10},{10,12},{12,14},{1,3},{3,5},{5,7},{... | collective-permute-start | bytes 331784 | tf_op jit(solution)/shard_map/ppermute | solution.py:26
  14.7 7.2 %collective-permute-start.1 = (f32[27,4,1,256]{3,0,2,1:T(8,128)S(1)}, f32[27,4,1,256]{3,0,2,1:T(8,128)S(1)}, u32[]{:S(2)}, u32[]{:S(2)}) collective-permute-start(f32[27,4,1,256]{3,0,2,1:T(8,128)S(1)} %copy.15), channel_id=1, source_target_pairs={{2,0},{4,2},{6,4},{8,6},{10,8},{12,10},{14,12},{3,1},{5,3},{7,5},{... | collective-permute-start | bytes 331784 | tf_op jit(solution)/shard_map/ppermute | solution.py:27
  23.7 26.9 %copy-start = (f32[27,4,32,256]{3,2,1,0:T(8,128)S(1)}, f32[27,4,32,256]{3,2,1,0:T(8,128)}, u32[]{:S(2)}) copy-start(f32[27,4,32,256]{3,2,1,0:T(8,128)} %param.3) | copy-start | bytes 10616836
  23.8 25.9 %collective-permute-start.2 = (f32[27,1,34,256]{3,2,1,0:T(8,128)S(1)}, f32[27,1,34,256]{3,2,1,0:T(8,128)S(1)}, u32[]{:S(2)}, u32[]{:S(2)}) collective-permute-start(f32[27,1,34,256]{3,2,1,0:T(8,128)S(1)} %get-tuple-element.8), channel_id=1, source_target_pairs={{1,0},{3,2},{5,4},{7,6},{9,8},{11,10},{13,12},{15,14},{17,16},{19,... | collective-permute-start | bytes 2820104 | tf_op jit(solution)/shard_map/ppermute | solution.py:27
  25.3 25.3 %collective-permute-start.3 = (f32[27,1,34,256]{3,2,1,0:T(8,128)S(1)}, f32[27,1,34,256]{3,2,1,0:T(8,128)S(1)}, u32[]{:S(2)}, u32[]{:S(2)}) collective-permute-start(f32[27,1,34,256]{3,2,1,0:T(8,128)S(1)} %get-tuple-element.9), channel_id=1, source_target_pairs={{0,1},{2,3},{4,5},{6,7},{8,9},{10,11},{12,13},{14,15},{16,17},{18,... | collective-permute-start | bytes 2820104 | tf_op jit(solution)/shard_map/ppermute | solution.py:26
  29.6 38.5 %copy-start.8 = (s32[256]{0:T(256)}, s32[256]{0:T(256)S(1)}, u32[]{:S(2)}) copy-start(s32[256]{0:T(256)S(1)} %iota_add_fusion) | copy-start | bytes 3076
  79.6 0.7 copy-start.11
  243.1 11.3 %copy-start.2 = (f32[3456,512]{1,0:T(8,128)S(1)}, f32[3456,512]{1,0:T(8,128)}, u32[]{:S(2)}) copy-start(f32[3456,512]{1,0:T(8,128)} %get-tuple-element.7) | copy-start | bytes 21233668
  243.1 11.3 %copy-start.7 = (pred[3456]{0:T(1024)(128)(4,1)S(1)}, pred[3456]{0:T(1024)(128)(4,1)}, u32[]{:S(2)}) copy-start(pred[3456]{0:T(1024)(128)(4,1)} %broadcast_in_dim.50) | copy-start | bytes 10372
  243.1 11.3 %copy-start.9 = (s32[256]{0:T(256)S(1)}, s32[256]{0:T(256)}, u32[]{:S(2)}) copy-start(s32[256]{0:T(256)} %copy-done.8) | copy-start | bytes 3076
  243.1 11.3 %copy-start.10 = (f32[512]{0:T(512)S(1)}, f32[512]{0:T(512)}, u32[]{:S(2)}) copy-start(f32[512]{0:T(512)} %fusion.40) | copy-start | bytes 6148
  254.4 8.4 %copy-start.3 = (f32[4,32,256]{2,1,0:T(8,128)S(1)}, f32[4,32,256]{2,1,0:T(8,128)}, u32[]{:S(2)}) copy-start(f32[4,32,256]{2,1,0:T(8,128)} %get-tuple-element.15) | copy-start | bytes 393220
  254.5 8.4 %copy-start.4 = (f32[4,32,256]{2,1,0:T(8,128)S(1)}, f32[4,32,256]{2,1,0:T(8,128)}, u32[]{:S(2)}) copy-start(f32[4,32,256]{2,1,0:T(8,128)} %get-tuple-element.18) | copy-start | bytes 393220
  254.5 8.4 %copy-start.5 = (f32[4,32,256]{2,1,0:T(8,128)S(1)}, f32[4,32,256]{2,1,0:T(8,128)}, u32[]{:S(2)}) copy-start(f32[4,32,256]{2,1,0:T(8,128)} %get-tuple-element.20) | copy-start | bytes 393220
  262.8 1.8 copy-start.1
Sparse Core Ops, SparseCore 0:
  79.8 163.3 all-reduce.3
where the time goes:
time: 297 us; the launch traced here: 295 us
  waiting for transfers between devices  182 us (61%)
  matrix products  42.8 us (14%)
  blocking collectives  21.9 us (7%)
  between operations  15 us (5%)
  starting transfers between devices  12.8 us (4%)
  other arithmetic  10.4 us (4%)
  local copies, waits for them, and re-layouts  9.33 us (3%)
    psum x1, waiting for transfers between devices, body(): cosine_part, sine_part = lax.psum((cosine_part, sine_part), 'phi')  157 us
    ppermute x2, waiting for transfers between devices, with_halo(): after = lax.ppermute(initial, axis, down)  24 us
    unnamed x1, blocking collectives  21.9 us
    dot_general x1, matrix products, body(): jnp.dot(field_lines, sin_table.T, precision=lax.Precision.HIGHEST)  11.7 us
    dot_general x1, matrix products, body(): jnp.dot(field_lines, cos_table.T, precision=lax.Precision.HIGHEST)  11.5 us
    dot_general x1, matrix products, body(): jnp.dot(cosine_part * weights, cos_table, precision=lax.Precision.HIGHEST)  11.3 us
    ppermute x2, starting transfers between devices, with_halo(): before = lax.ppermute(last, axis, up)  9.91 us
    dot_general x1, matrix products, body(): jnp.dot(sine_part * weights, sin_table, precision=lax.Precision.HIGHEST)  8.31 us
  transfers between devices with their start and end apart: 5, of which 5 were waited for; matrix products, arithmetic and copies ran while one was open for 2% of the time, Pallas kernels for 0%

commit v1 on v0

v1 whole, which is shorter than its diff:
```python
import functools
import math

import jax
import jax.numpy as jnp
import ml_dtypes
import numpy as np
from jax import lax
from jax.experimental import pallas as pl
from jax.experimental.pallas import tpu as pltpu
from jax.sharding import PartitionSpec as P

MESH = pl.DeviceIdType.MESH
NPHI = 2048
MMAX = 512
STAGES = 9
PHI = 8
F32 = jnp.float32
BF16 = jnp.bfloat16


def split_bf16(a):
    hi = a.astype(ml_dtypes.bfloat16)
    lo = (a - hi.astype(np.float64)).astype(ml_dtypes.bfloat16)
    return np.stack([hi, lo])


def fourier_constants():
    cell = np.arange(256)
    block = np.arange(64)

    def tables(mode):
        angle = 2.0 * math.pi * ((cell[:, None] * mode[None, :]) % NPHI) / NPHI
        return np.cos(angle), np.sin(angle)

    def scale(mode):
        return np.where(mode == 0, 1.0 / NPHI, 2.0 / NPHI)

    forward, inverse, modes = [], [], []
    singles, singles_back = [], []
    for r in (0, 4):
        mode = 8 * block + r
        c, s = tables(mode)
        full = np.concatenate([c, s], axis=1)
        singles.append(full)
        singles_back.append((full * np.tile(scale(mode), 2)).T)
        modes.append(np.tile(mode, 2))
    modes = [np.concatenate(modes)]
    for r in (1, 2, 3):
        m, n = 8 * block + r, 8 * block + 8 - r
        cm, sm = tables(m)
        cn, sn = tables(n)
        upper = np.concatenate([cm, sm, cn, sn], axis=1)
        lower = np.concatenate([-sm, cm, sn, -cn], axis=1)
        full = np.concatenate([upper, lower], axis=0)
        weights = np.concatenate([scale(m), scale(m), scale(n), scale(n)])
        forward.append(full)
        inverse.append((full * weights).T)
        modes.append(np.concatenate([m, m, n, n]))
    modes = np.broadcast_to(np.stack(modes).astype(np.float32)[:, None, :], (4, 8, 256))
    return (
        split_bf16(np.stack(forward)),
        split_bf16(np.stack(inverse)),
        split_bf16(np.stack(singles)),
        split_bf16(np.stack(singles_back)),
        np.ascontiguousarray(modes),
    )


def row_tables():
    j = np.arange(256)
    d = math.pi / 256
    angle = d * (j + 0.5)
    south = np.sin(angle + 0.5 * d) / np.sin(angle)
    north = np.sin(angle - 0.5 * d) / np.sin(angle)
    polar = (3 * (2 * j + 1) < 256) | (3 * (2 * (255 - j) + 1) < 256)
    kinds = np.stack([south, north, np.cos(angle), np.sin(angle), polar.astype(np.float64)])
    kinds = kinds.reshape(5, 8, 32).transpose(1, 0, 2)
    return np.ascontiguousarray(np.broadcast_to(kinds[..., None], (8, 5, 32, 128)).astype(np.float32))


def radial_constants():
    h = 0.3 / 8
    r = 0.7 + h * (np.arange(8) + 0.5)
    return ((r + h / 2) / r) ** 2, ((r - h / 2) / r) ** 2, (1.0 / r) ** 2


def split_rows(a):
    hi = a.astype(BF16).astype(F32)
    return jnp.concatenate([hi, a - hi], axis=0).astype(BF16)


def dot(a, b):
    return jnp.dot(a, b, preferred_element_type=F32)


def dot_split(a, high, low):
    lines = a.shape[0]
    both = split_rows(a)
    out = dot(both, high) + dot(both, low)
    return out[:lines] + out[lines:]


def filter_lines(blocks, keep, modes, fwd, inv, one, back):
    x0, x1, x2, x3, x4, x5, x6, x7 = blocks
    half = math.sqrt(0.5)
    s04, d04, s26, d26 = x0 + x4, x0 - x4, x2 + x6, x2 - x6
    s15, d15, s37, d37 = x1 + x5, x1 - x5, x3 + x7, x3 - x7
    even, odd = s04 + s26, s15 + s37
    cross, plus = half * (d15 - d37), half * (d15 + d37)
    pairs = [(d04 + cross, d26 + plus), (s04 - s26, s15 - s37), (d04 - cross, plus - d26)]

    def masked(mid, group):
        lines = mid.shape[0]
        kept = mid.reshape(lines // 8, 8, 256)
        kept = jnp.where((modes[group] < keep)[None], kept, 0.0)
        return kept.reshape(lines, 256)

    mid = jnp.concatenate(
        [dot_split(even + odd, one[0, 0], one[1, 0]), dot_split(even - odd, one[0, 1], one[1, 1])], axis=1
    )
    mid = masked(mid, 0)
    p0 = dot_split(mid[:, :128], back[0, 0], back[1, 0])
    p4 = dot_split(mid[:, 128:], back[0, 1], back[1, 1])
    p, q = [], []
    for r, (u, v) in enumerate(pairs):
        mid = dot_split(jnp.concatenate([u, v], axis=1), fwd[0, r], fwd[1, r])
        mid = masked(mid, r + 1)
        out = dot_split(mid, inv[0, r], inv[1, r])
        p.append(out[:, :256])
        q.append(out[:, 256:])
    (p1, p2, p3), (q1, q2, q3) = p, q
    a, b = p0 + p4, p0 - p4
    p13, q13 = p1 + p3, q1 - q3
    ph, qh = half * (p1 - p3), half * (q1 + q3)
    ap, am, bp, bm = a + p2, a - p2, b + q2, b - q2
    return [
        ap + p13,
        bp + (ph + qh),
        am + q13,
        bm - (ph - qh),
        ap - p13,
        bp - (ph + qh),
        am - q13,
        bm + (ph - qh),
    ]


def kernel(
    tf, vel, kept, tab_hbm, fwd_hbm, inv_hbm, one_hbm, back_hbm, modes_hbm,
    out, emf,
    xp, v, tab, fwd, inv, one, back, modes,
    edge, halo_t, halo_r, coef, keep, st, rx, yb, res, acc, got,
    load_sem, theta_send, theta_recv, row_send, row_recv, keep_send, keep_recv,
    a_send, a_recv, b_send, b_recv, out_sem, emf_send, emf_recv,
):
    phi, theta, row = lax.axis_index("phi"), lax.axis_index("theta"), lax.axis_index("row")
    heavy = (theta == 0) | (theta == 7)
    light = (theta == 1) | (theta == 6)
    helper = (theta == 2) | (theta == 5)
    source = heavy | light
    worker = source | helper
    partner = jnp.where(theta == 0, 2, jnp.where(theta == 2, 0, jnp.where(theta == 7, 5, 7)))
    octet = jnp.where(helper | (theta == 6), 2, 0)
    my_i, my_o = phi // 2, octet + phi % 2

    def others(k):
        return lax.rem(phi + k, PHI)

    loads = [
        pltpu.make_async_copy(tf, xp.at[:, :, pl.ds(8, 32), :], load_sem.at[0]),
        pltpu.make_async_copy(vel, v, load_sem.at[1]),
        pltpu.make_async_copy(tab_hbm.at[theta], tab, load_sem.at[2]),
        pltpu.make_async_copy(fwd_hbm, fwd, load_sem.at[3]),
        pltpu.make_async_copy(inv_hbm, inv, load_sem.at[4]),
        pltpu.make_async_copy(one_hbm, one, load_sem.at[5]),
        pltpu.make_async_copy(back_hbm, back, load_sem.at[6]),
        pltpu.make_async_copy(modes_hbm, modes, load_sem.at[7]),
    ]
    for load in loads:
        load.start()

    barrier = pltpu.get_barrier_semaphore()
    pl.semaphore_signal(barrier, inc=1, device_id={"row": 1 - row}, device_id_type=MESH)
    for k in range(1, PHI):
        pl.semaphore_signal(barrier, inc=1, device_id={"phi": others(k)}, device_id_type=MESH)

    @pl.when(theta > 0)
    def _():
        pl.semaphore_signal(barrier, inc=1, device_id={"theta": theta - 1}, device_id_type=MESH)

    @pl.when(theta < 7)
    def _():
        pl.semaphore_signal(barrier, inc=1, device_id={"theta": theta + 1}, device_id_type=MESH)

    @pl.when(heavy | helper)
    def _():
        for k in range(PHI):
            pl.semaphore_signal(
                barrier, inc=1, device_id={"theta": partner, "phi": others(k)}, device_id_type=MESH
            )

    loads[0].wait()

    def pack(f, _):
        for i in range(4):
            edge[0, f, pl.ds(i, 1), :] = xp[f, i, pl.ds(8, 1), :]
            edge[1, f, pl.ds(i, 1), :] = xp[f, i, pl.ds(39, 1), :]
        return 0

    lax.fori_loop(0, 27, pack, 0)
    eye = lax.broadcasted_iota(jnp.int32, (32, 32), 0) == lax.broadcasted_iota(jnp.int32, (32, 32), 1)
    counts = jnp.where(eye, jnp.broadcast_to(kept[...], (32, 32)), 0).astype(F32)
    keep[0] = jnp.broadcast_to(jnp.sum(counts, axis=1, keepdims=True), (32, 128))

    peers = PHI + jnp.where(theta > 0, 1, 0) + jnp.where(theta < 7, 1, 0) + jnp.where(heavy | helper, PHI, 0)
    pl.semaphore_wait(barrier, peers)

    def theta_copy(side, there):
        return pltpu.make_async_remote_copy(
            src_ref=edge.at[side], dst_ref=halo_t.at[side], send_sem=theta_send.at[side],
            recv_sem=theta_recv.at[side], device_id={"theta": there}, device_id_type=MESH)

    @pl.when(theta > 0)
    def _():
        theta_copy(0, theta - 1).start()

    @pl.when(theta < 7)
    def _():
        theta_copy(1, theta + 1).start()

    keep_copy = pltpu.make_async_remote_copy(
        src_ref=keep.at[0], dst_ref=keep.at[1], send_sem=keep_send, recv_sem=keep_recv,
        device_id={"theta": partner}, device_id_type=MESH)

    @pl.when(heavy)
    def _():
        keep_copy.start()

    edge_i = jnp.where(row == 0, 3, 0)

    def row_copy(n):
        return pltpu.make_async_remote_copy(
            src_ref=xp.at[pl.ds(3 * n, 3), edge_i, pl.ds(8, 32), :], dst_ref=halo_r.at[pl.ds(3 * n, 3)],
            send_sem=row_send, recv_sem=row_recv.at[n],
            device_id={"row": 1 - row}, device_id_type=MESH)

    def send_row(n, _):
        row_copy(n).start()
        return 0

    lax.fori_loop(0, STAGES, send_row, 0)

    for load in loads[1:]:
        load.wait()
    outward, inward, metric = radial_constants()

    def radial(values, i):
        return jnp.where(row == 0, F32(values[i]), F32(values[i + 4]))

    south, north = tab[0], tab[1]
    for i in range(4):
        g = 0.1 * radial(metric, i)
        cs, cn = g * south, g * north
        both = 0.2 * (radial(outward, i) + radial(inward, i))
        centre = (1.0 - both) - (cs + cn)
        for lanes in range(2):
            part = pl.ds(128 * lanes, 128)
            coef[0, i, :, part] = cs
            coef[1, i, :, part] = cn
            coef[2, i, :, part] = centre

    @pl.when(theta < 7)
    def _():
        theta_copy(0, theta).wait_recv()

    @pl.when(theta > 0)
    def _():
        theta_copy(1, theta).wait_recv()

    @pl.when(theta == 7)
    def _():
        halo_t[0] = jnp.zeros((27, 4, 256), F32)

    @pl.when(theta == 0)
    def _():
        halo_t[1] = jnp.zeros((27, 4, 256), F32)

    inner = jnp.where(row == 1, F32(1.0), F32(0.0))
    outer = jnp.where(row == 0, F32(1.0), F32(0.0))

    def a_copy(n, k, there, o_base, sem):
        p = others(k)
        i, o = p // 2, o_base + p % 2
        return pltpu.make_async_remote_copy(
            src_ref=st.at[pl.ds(3 * n, 3), i, pl.ds(pl.multiple_of(o * 8, 8), 8), :],
            dst_ref=rx.at[n, phi], send_sem=a_send.at[sem], recv_sem=a_recv.at[n],
            device_id={"theta": there, "phi": p}, device_id_type=MESH)

    def step(n, _):
        p_unit, q_unit = n // 3, n % 3
        row_copy(n).wait_recv()
        unit = [jnp.where(p_unit == k, F32(0.5), F32(0.0)) for k in range(3)]
        weight = [jnp.where(q_unit == k, F32(1.0), F32(0.0)) for k in range(3)]
        profile = weight[0] + weight[1] * tab[2] + weight[2] * tab[3]
        profile = jnp.concatenate([profile, profile], axis=1)
        for c in range(3):
            f = 3 * n + c
            for i in range(4):
                xp[f, i, pl.ds(7, 1), :] = halo_t[1, f, pl.ds(i, 1), :]
                xp[f, i, pl.ds(40, 1), :] = halo_t[0, f, pl.ds(i, 1), :]
        for i in range(4):
            v0, v1, v2 = v[0, i], v[1, i], v[2, i]
            turned = (v1 * unit[2] - v2 * unit[1], v2 * unit[0] - v0 * unit[2], v0 * unit[1] - v1 * unit[0])
            for c in range(3):
                f = 3 * n + c
                b = xp[f, i, pl.ds(8, 32), :]
                up = xp[f, i + 1, pl.ds(8, 32), :] if i < 3 else halo_r[f]
                down = xp[f, i - 1, pl.ds(8, 32), :] if i > 0 else halo_r[f]
                cu, cd = 0.2 * radial(outward, i), 0.2 * radial(inward, i)
                if i == 3:
                    cu = cu * outer
                if i == 0:
                    cd = cd * inner
                total = coef[2, i] * b + cu * up + cd * down + profile * turned[c]
                total = total + coef[0, i] * xp[f, i, pl.ds(9, 32), :] + coef[1, i] * xp[f, i, pl.ds(7, 32), :]
                st[f, i] = total

        @pl.when(source)
        def _():
            pltpu.make_async_copy(
                st.at[pl.ds(3 * n, 3), my_i, pl.ds(pl.multiple_of(my_o * 8, 8), 8), :], rx.at[n, phi], a_recv.at[n]
            ).start()
            for k in range(1, PHI):
                a_copy(n, k, theta, octet, 0).start()

        @pl.when(heavy)
        def _():
            for k in range(PHI):
                a_copy(n, k, partner, 2, 1).start()

        @pl.when(light)
        def _():
            rest = pl.ds(pl.multiple_of(16 - 8 * octet, 8), 16)
            for c in range(3):
                res[3 * n + c, :, rest, :] = st[3 * n + c, :, rest, :]

        @pl.when(jnp.logical_not(source))
        def _():
            for c in range(3):
                res[3 * n + c] = st[3 * n + c]

        return 0

    lax.fori_loop(0, STAGES, step, 0)

    home = jnp.where(helper, partner, theta)

    def b_copy(n, p):
        return pltpu.make_async_remote_copy(
            src_ref=yb.at[n, p],
            dst_ref=res.at[pl.ds(3 * n, 3), my_i, pl.ds(pl.multiple_of(my_o * 8, 8), 8), :],
            send_sem=b_send, recv_sem=b_recv.at[n],
            device_id={"theta": home, "phi": p}, device_id_type=MESH)

    @pl.when(worker)
    def _():
        @pl.when(helper)
        def _():
            keep_copy.wait_recv()

        mine = pl.ds(pl.multiple_of(my_o * 8, 8), 8)
        which = jnp.where(helper, 1, 0)
        kept_rows = keep[which, mine, :]
        kept_rows = jnp.concatenate([kept_rows, kept_rows], axis=1)
        polar = jnp.maximum(tab[4, mine, :], jnp.where(helper, F32(1.0), F32(0.0)))
        polar = jnp.concatenate([polar, polar], axis=1) > 0.5

        def work(n, _):
            pltpu.make_async_copy(rx.at[n], rx.at[n], a_recv.at[n]).wait()
            blocks = [rx[n, p].reshape(24, 256) for p in range(PHI)]
            done = filter_lines(blocks, kept_rows, modes, fwd, inv, one, back)
            for p in range(PHI):
                yb[n, p] = jnp.where(polar[None], done[p].reshape(3, 8, 256), rx[n, p])

            for k in range(1, PHI):
                b_copy(n, others(k)).start()

            @pl.when(helper)
            def _():
                b_copy(n, phi).start()

            @pl.when(source)
            def _():
                pltpu.make_async_copy(
                    yb.at[n, phi],
                    res.at[pl.ds(3 * n, 3), my_i, pl.ds(pl.multiple_of(my_o * 8, 8), 8), :],
                    b_recv.at[n],
                ).start()

            return 0

        lax.fori_loop(0, STAGES, work, 0)

    acc[...] = jnp.zeros((32, 128), F32)
    lane = lax.broadcasted_iota(jnp.int32, (32, 128), 1)

    def out_copy(n):
        return pltpu.make_async_copy(res.at[pl.ds(3 * n, 3)], out.at[pl.ds(3 * n, 3)], out_sem.at[n])

    def finish(n, _):
        @pl.when(heavy)
        def _():
            whole = res.at[pl.ds(3 * n, 3)]
            pltpu.make_async_copy(whole, whole, b_recv.at[n]).wait()

        @pl.when(light)
        def _():
            part = res.at[pl.ds(3 * n, 3), :, pl.ds(pl.multiple_of(octet * 8, 8), 16), :]
            pltpu.make_async_copy(part, part, b_recv.at[n]).wait()

        out_copy(n).start()
        total = acc[...]
        for i in range(4):
            v0, v1, v2 = v[0, i], v[1, i], v[2, i]
            r0, r1, r2 = res[3 * n, i], res[3 * n + 1, i], res[3 * n + 2, i]
            terms = (v1 * r2 - v2 * r1, v2 * r0 - v0 * r2, v0 * r1 - v1 * r0)
            for c in range(3):
                summed = jnp.sum(terms[c][:, :128] + terms[c][:, 128:], axis=1, keepdims=True)
                total = jnp.where(lane == 4 * (3 * n + c) + i, jnp.broadcast_to(summed, (32, 128)), total)
        acc[...] = total
        return 0

    lax.fori_loop(0, STAGES, finish, 0)

    def emf_copy(k):
        p = others(k)
        return pltpu.make_async_remote_copy(
            src_ref=acc.at[pl.ds(pl.multiple_of(p // 2 * 8, 8), 8), :], dst_ref=got.at[phi],
            send_sem=emf_send, recv_sem=emf_recv, device_id={"phi": p}, device_id_type=MESH)

    for k in range(1, PHI):
        emf_copy(k).start()
    pltpu.make_async_copy(acc.at[pl.ds(pl.multiple_of(phi // 2 * 8, 8), 8), :], got.at[phi], emf_recv).start()
    pltpu.make_async_copy(got, got, emf_recv).wait()
    summed = got[0]
    for p in range(1, PHI):
        summed = summed + got[p]
    summed = summed * (1.0 / NPHI)
    emf[...] = jnp.where(phi % 2 == 0, summed[:4], summed[4:])

    def drain(ref, sem):
        pltpu.make_async_copy(ref, ref, sem).wait()

    seven = got.at[pl.ds(0, 7)]
    drain(seven, emf_send)
    drain(halo_r, row_send)

    @pl.when(theta > 0)
    def _():
        theta_copy(0, theta).wait_send()

    @pl.when(theta < 7)
    def _():
        theta_copy(1, theta).wait_send()

    @pl.when(heavy)
    def _():
        keep_copy.wait_send()
        drain(rx, a_send.at[1])

    @pl.when(source)
    def _():
        drain(rx.at[:, pl.ds(0, 7)], a_send.at[0])
        drain(yb.at[:, pl.ds(0, 7)], b_send)

    @pl.when(helper)
    def _():
        drain(yb, b_send)

    def drain_out(n, _):
        out_copy(n).wait()
        return 0

    lax.fori_loop(0, STAGES, drain_out, 0)


def body(test_fields, velocity, kept):
    forward, inverse, singles, singles_back, modes = fourier_constants()
    tables = row_tables()
    hbm, vmem = pl.BlockSpec(memory_space=pl.ANY), pl.BlockSpec(memory_space=pltpu.VMEM)
    dma, regular = pltpu.SemaphoreType.DMA, pltpu.SemaphoreType.REGULAR
    del regular
    result, emf = pl.pallas_call(
        kernel,
        out_shape=(
            jax.ShapeDtypeStruct((27, 4, 32, 256), F32),
            jax.ShapeDtypeStruct((4, 128), F32),
        ),
        in_specs=[hbm, hbm, vmem] + [hbm] * 6,
        out_specs=(hbm, vmem),
        scratch_shapes=[
            pltpu.VMEM((27, 4, 48, 256), F32),
            pltpu.VMEM((3, 4, 32, 256), F32),
            pltpu.VMEM((5, 32, 128), F32),
            pltpu.VMEM(forward.shape, BF16),
            pltpu.VMEM(inverse.shape, BF16),
            pltpu.VMEM(singles.shape, BF16),
            pltpu.VMEM(singles_back.shape, BF16),
            pltpu.VMEM(modes.shape, F32),
            pltpu.VMEM((2, 27, 4, 256), F32),
            pltpu.VMEM((2, 27, 4, 256), F32),
            pltpu.VMEM((27, 32, 256), F32),
            pltpu.VMEM((3, 4, 32, 256), F32),
            pltpu.VMEM((2, 32, 128), F32),
            pltpu.VMEM((27, 4, 32, 256), F32),
            pltpu.VMEM((STAGES, PHI, 3, 8, 256), F32),
            pltpu.VMEM((STAGES, PHI, 3, 8, 256), F32),
            pltpu.VMEM((27, 4, 32, 256), F32),
            pltpu.VMEM((32, 128), F32),
            pltpu.VMEM((PHI, 8, 128), F32),
            dma((8,)),
            dma((2,)),
            dma((2,)),
            dma,
            dma((STAGES,)),
            dma,
            dma,
            dma((2,)),
            dma((STAGES,)),
            dma,
            dma((STAGES,)),
            dma((STAGES,)),
            dma,
            dma,
        ],
        compiler_params=pltpu.CompilerParams(
            collective_id=0, has_side_effects=True, vmem_limit_bytes=48 * 2**20
        ),
        name="substep",
    )(
        test_fields, velocity, kept.reshape(1, 32), jnp.asarray(tables), jnp.asarray(forward),
        jnp.asarray(inverse), jnp.asarray(singles), jnp.asarray(singles_back), jnp.asarray(modes),
    )
    emf = emf[:, :108].T.reshape(27, 4, 4)
    return result, emf


def solution(mesh):
    return jax.shard_map(
        body,
        mesh=mesh,
        in_specs=(P(None, "row", "theta", "phi"), P(None, "row", "theta", "phi"), P("theta")),
        out_specs=(P(None, "row", "theta", "phi"), P(None, "row", ("theta", "phi"))),
        check_vma=False,
    )
```

time: 297 us -> 94.3 us (0.32)
  waiting for transfers between devices: 182 us -> 0 us
  Pallas kernels: 0 us -> 79.9 us
  matrix products: 42.8 us -> 0 us
  blocking collectives: 21.9 us -> 0 us
  between operations: 15 us -> 0.67 us
  starting transfers between devices: 12.8 us -> 0 us
  other arithmetic: 10.4 us -> 0 us
  local copies, waits for them, and re-layouts: 9.33 us -> 13.3 us
    psum x1 -> x0, waiting for transfers between devices: 157 us -> none  [body(): cosine_part, sine_part = lax.psum((cosine_part, sine_part), 'phi')]
    pallas_call x0 -> x1, Pallas kernels: none -> 79.9 us  [body(): pl.pallas_call(kernel, out_shape=(jax.ShapeDtypeStruct((27, 4, 32, 256),...]
    dot_general x4 -> x0, matrix products: 42.8 us -> none  [the longest x1 11.7 us: body(): jnp.dot(field_lines, sin_table.T, precision=lax.Precision.HIGHEST)]
    ppermute x4 -> x0, waiting for transfers between devices: 25.6 us -> none  [the longest x2 24 us: with_halo(): after = lax.ppermute(initial, axis, down)]
    unnamed x1 -> x0, blocking collectives: 21.9 us -> none
    ppermute x4 -> x0, starting transfers between devices: 12.8 us -> none  [the longest x2 9.91 us: with_halo(): before = lax.ppermute(last, axis, up)]
    unnamed x29 -> x18, local copies, waits for them, and re-layouts: 3.79 us -> 13.2 us
    add x2 -> x0, other arithmetic: 5.75 us -> none  [the longest x1 5.74 us: body(): test_fields + diffuse(padded, outward, inward, metric, north_side, south_...]
  transfers between devices with their start and end apart: 5 -> 0, of which waited for: 5 -> 0; matrix products, arithmetic and copies ran while one was open for 2% -> 0% of each run, Pallas kernels for 0% -> 0%
where the time goes in v1:
time: 94.3 us; the launch traced here: 93.9 us
  Pallas kernels  79.9 us (85%)
  local copies, waits for them, and re-layouts  13.3 us (14%)
    pallas_call x1, Pallas kernels, body(): pl.pallas_call(kernel, out_shape=(jax.ShapeDtypeStruct((27, 4, 32, 256),...  79.9 us
    unnamed x18, local copies, waits for them, and re-layouts  13.2 us

profile of v1, /device:TPU:1, one launch (start us, length us, event | category | flops | bytes accessed | tf_op | source)
XLA Modules:
  0.0 93.9 jit_solution(15551090810077758465)
XLA Ops:
  0.6 0.0 copy-start
  0.6 1.4 %copy-done = bf16[2,3,256,512]{3,2,1,0:T(8,128)(2,1)S(1)} copy-done((bf16[2,3,256,512]{3,2,1,0:T(8,128)(2,1)S(1)}, bf16[2,3,256,512]{3,2,1,0:T(8,128)(2,1)}, u32[]{:S(2)}) %copy-start) | copy-done | bytes 1572888
  2.0 0.0 copy-start.1
  2.0 1.4 %copy-done.1 = bf16[2,3,512,256]{3,2,1,0:T(8,128)(2,1)S(1)} copy-done((bf16[2,3,512,256]{3,2,1,0:T(8,128)(2,1)S(1)}, bf16[2,3,512,256]{3,2,1,0:T(8,128)(2,1)}, u32[]{:S(2)}) %copy-start.1) | copy-done | bytes 1572888
  3.5 0.0 copy-start.2
  3.5 1.1 %copy-done.2 = f32[8,5,32,128]{3,2,1,0:T(8,128)S(1)} copy-done((f32[8,5,32,128]{3,2,1,0:T(8,128)S(1)}, f32[8,5,32,128]{3,2,1,0:T(8,128)}, u32[]{:S(2)}) %copy-start.2) | copy-done | bytes 655384
  4.5 0.0 copy-start.3
  4.5 1.0 %copy-done.3 = f32[3,4,32,256]{3,2,1,0:T(8,128)S(1)} copy-done((f32[3,4,32,256]{3,2,1,0:T(8,128)S(1)}, f32[3,4,32,256]{3,2,1,0:T(8,128)}, u32[]{:S(2)}) %copy-start.3) | copy-done | bytes 393240
  5.5 0.0 copy-start.4
  5.5 0.9 %copy-done.4 = bf16[2,2,128,256]{3,2,1,0:T(8,128)(2,1)S(1)} copy-done((bf16[2,2,128,256]{3,2,1,0:T(8,128)(2,1)S(1)}, bf16[2,2,128,256]{3,2,1,0:T(8,128)(2,1)}, u32[]{:S(2)}) %copy-start.4) | copy-done | bytes 262168
  6.5 0.0 copy-start.5
  6.5 0.9 %copy-done.5 = bf16[2,2,256,128]{3,2,1,0:T(8,128)(2,1)S(1)} copy-done((bf16[2,2,256,128]{3,2,1,0:T(8,128)(2,1)S(1)}, bf16[2,2,256,128]{3,2,1,0:T(8,128)(2,1)}, u32[]{:S(2)}) %copy-start.5) | copy-done | bytes 262168
  7.4 0.0 copy-start.6
  7.4 0.8 copy-done.6
  8.2 0.0 copy-start.7
  8.2 0.7 copy-done.7
  8.8 79.9 %substep.1 = (f32[27,4,32,256]{3,2,1,0:T(8,128)}, f32[4,128]{1,0:T(4,128)S(1)}) custom-call(f32[27,4,32,256]{3,2,1,0:T(8,128)} %tf.1, f32[3,4,32,256]{3,2,1,0:T(8,128)S(1)} %copy-done.3, s32[1,32]{1,0:T(1,128)S(1)} %bitcast.5, f32[8,5,32,128]{3,2,1,0:T(8,128)S(1)} %copy-done.2, bf16[2,3,512,256]{3,2,1,0:T(8,128)(2,1)S(1)} %copy-done.1, ...), custom_call_target="tpu_custom_call" | custom-call | tf_op jit(solution)/shard_map/substep/pallas_call | solution.py:494
  88.8 0.1 reshape.11
  88.9 0.7 copy.12
  89.6 4.3 %copy.14 = f32[27,4,32,256]{3,2,1,0:T(8,128)} copy(f32[27,4,32,256]{3,2,1,0:T(8,128)} %get-tuple-element.12) | data formatting | bytes 7077888
  (1 shorter events, 0.0 us)
Async XLA Ops:
  0.6 1.4 %copy-start = (bf16[2,3,256,512]{3,2,1,0:T(8,128)(2,1)S(1)}, bf16[2,3,256,512]{3,2,1,0:T(8,128)(2,1)}, u32[]{:S(2)}) copy-start(bf16[2,3,256,512]{3,2,1,0:T(8,128)(2,1)} %constant.14.clone.inv_hbm) | copy-start | bytes 4718596
  2.0 1.4 %copy-start.1 = (bf16[2,3,512,256]{3,2,1,0:T(8,128)(2,1)S(1)}, bf16[2,3,512,256]{3,2,1,0:T(8,128)(2,1)}, u32[]{:S(2)}) copy-start(bf16[2,3,512,256]{3,2,1,0:T(8,128)(2,1)} %constant.13.clone.fwd_hbm) | copy-start | bytes 4718596
  3.5 1.1 %copy-start.2 = (f32[8,5,32,128]{3,2,1,0:T(8,128)S(1)}, f32[8,5,32,128]{3,2,1,0:T(8,128)}, u32[]{:S(2)}) copy-start(f32[8,5,32,128]{3,2,1,0:T(8,128)} %constant.12.clone.tab_hbm) | copy-start | bytes 1966084
  4.5 1.0 %copy-start.3 = (f32[3,4,32,256]{3,2,1,0:T(8,128)S(1)}, f32[3,4,32,256]{3,2,1,0:T(8,128)}, u32[]{:S(2)}) copy-start(f32[3,4,32,256]{3,2,1,0:T(8,128)} %vel.1) | copy-start | bytes 1179652
  5.5 0.9 %copy-start.4 = (bf16[2,2,128,256]{3,2,1,0:T(8,128)(2,1)S(1)}, bf16[2,2,128,256]{3,2,1,0:T(8,128)(2,1)}, u32[]{:S(2)}) copy-start(bf16[2,2,128,256]{3,2,1,0:T(8,128)(2,1)} %constant.16.clone.back_hbm) | copy-start | bytes 786436
  6.5 0.9 %copy-start.5 = (bf16[2,2,256,128]{3,2,1,0:T(8,128)(2,1)S(1)}, bf16[2,2,256,128]{3,2,1,0:T(8,128)(2,1)}, u32[]{:S(2)}) copy-start(bf16[2,2,256,128]{3,2,1,0:T(8,128)(2,1)} %constant.15.clone.one_hbm) | copy-start | bytes 786436
  7.4 0.8 copy-start.6
  8.2 0.7 copy-start.7

commit v2 on v1

--- a/solution.py
+++ b/solution.py
@@ -14,6 +14,11 @@
 NPHI = 2048
 MMAX = 512
 STAGES = 9
+AHEAD = 2
+ACROSS = 2
+LAG = 4
+BEHIND = 1
+HELP = 0
 PHI = 8
 F32 = jnp.float32
 BF16 = jnp.bfloat16
@@ -150,9 +155,9 @@
     tf, vel, kept, tab_hbm, fwd_hbm, inv_hbm, one_hbm, back_hbm, modes_hbm,
     out, emf,
     xp, v, tab, fwd, inv, one, back, modes,
-    edge, halo_t, halo_r, coef, keep, st, rx, yb, res, acc, got,
+    edge, halo_t, halo_r, coef, keep, st, rx, yb, res, rel, acc, got,
     load_sem, theta_send, theta_recv, row_send, row_recv, keep_send, keep_recv,
-    a_send, a_recv, b_send, b_recv, out_sem, emf_send, emf_recv,
+    a_send, across_send, a_recv, b_send, b_recv, rel_send, rel_recv, out_sem, emf_send, emf_recv,
 ):
     phi, theta, row = lax.axis_index("phi"), lax.axis_index("theta"), lax.axis_index("row")
     heavy = (theta == 0) | (theta == 7)
@@ -242,14 +247,11 @@
     def row_copy(n):
         return pltpu.make_async_remote_copy(
             src_ref=xp.at[pl.ds(3 * n, 3), edge_i, pl.ds(8, 32), :], dst_ref=halo_r.at[pl.ds(3 * n, 3)],
-            send_sem=row_send, recv_sem=row_recv.at[n],
+            send_sem=row_send.at[n], recv_sem=row_recv.at[n],
             device_id={"row": 1 - row}, device_id_type=MESH)
 
-    def send_row(n, _):
+    for n in range(AHEAD):
         row_copy(n).start()
-        return 0
-
-    lax.fori_loop(0, STAGES, send_row, 0)
 
     for load in loads[1:]:
         load.wait()
@@ -289,17 +291,29 @@
     inner = jnp.where(row == 1, F32(1.0), F32(0.0))
     outer = jnp.where(row == 0, F32(1.0), F32(0.0))
 
+    def drain(ref, sem):
+        pltpu.make_async_copy(ref, ref, sem).wait()
+
     def a_copy(n, k, there, o_base, sem):
         p = others(k)
         i, o = p // 2, o_base + p % 2
         return pltpu.make_async_remote_copy(
             src_ref=st.at[pl.ds(3 * n, 3), i, pl.ds(pl.multiple_of(o * 8, 8), 8), :],
-            dst_ref=rx.at[n, phi], send_sem=a_send.at[sem], recv_sem=a_recv.at[n],
+            dst_ref=rx.at[n, phi], send_sem=sem, recv_sem=a_recv.at[n],
             device_id={"theta": there, "phi": p}, device_id_type=MESH)
 
-    def step(n, _):
+    def across_copy(n, k):
+        return a_copy(n, k, partner, 2, across_send.at[lax.rem(n, ACROSS)])
+
+    def step(n):
         p_unit, q_unit = n // 3, n % 3
         row_copy(n).wait_recv()
+        row_copy(n).wait_send()
+
+        @pl.when(n + AHEAD < STAGES)
+        def _():
+            row_copy(n + AHEAD).start()
+
         unit = [jnp.where(p_unit == k, F32(0.5), F32(0.0)) for k in range(3)]
         weight = [jnp.where(q_unit == k, F32(1.0), F32(0.0)) for k in range(3)]
         profile = weight[0] + weight[1] * tab[2] + weight[2] * tab[3]
@@ -332,12 +346,16 @@
                 st.at[pl.ds(3 * n, 3), my_i, pl.ds(pl.multiple_of(my_o * 8, 8), 8), :], rx.at[n, phi], a_recv.at[n]
             ).start()
             for k in range(1, PHI):
-                a_copy(n, k, theta, octet, 0).start()
+                a_copy(n, k, theta, octet, a_send).start()
 
         @pl.when(heavy)
         def _():
+            @pl.when(n >= ACROSS)
+            def _():
+                drain(rx.at[0], across_send.at[lax.rem(n, ACROSS)])
+
             for k in range(PHI):
-                a_copy(n, k, partner, 2, 1).start()
+                across_copy(n, k).start()
 
         @pl.when(light)
         def _():
@@ -349,58 +367,60 @@
         def _():
             for c in range(3):
                 res[3 * n + c] = st[3 * n + c]
-
-        return 0
-
-    lax.fori_loop(0, STAGES, step, 0)
-
-    home = jnp.where(helper, partner, theta)
 
     def b_copy(n, p):
         return pltpu.make_async_remote_copy(
             src_ref=yb.at[n, p],
             dst_ref=res.at[pl.ds(3 * n, 3), my_i, pl.ds(pl.multiple_of(my_o * 8, 8), 8), :],
             send_sem=b_send, recv_sem=b_recv.at[n],
-            device_id={"theta": home, "phi": p}, device_id_type=MESH)
-
-    @pl.when(worker)
-    def _():
-        @pl.when(helper)
+            device_id={"phi": p}, device_id_type=MESH)
+
+    relay_rows = pl.ds(pl.multiple_of(phi % 2 * 8, 8), 8)
+
+    def gather_copy(n, p):
+        return pltpu.make_async_remote_copy(
+            src_ref=yb.at[n, p], dst_ref=rel.at[n, :, my_i, relay_rows, :],
+            send_sem=b_send, recv_sem=rel_recv.at[n], device_id={"phi": p}, device_id_type=MESH)
+
+    def relay(n):
+        pltpu.make_async_copy(rel.at[n], rel.at[n], rel_recv.at[n]).wait()
+        pltpu.make_async_remote_copy(
+            src_ref=rel.at[n], dst_ref=res.at[pl.ds(3 * n, 3), :, pl.ds(16, 16), :],
+            send_sem=rel_send, recv_sem=b_recv.at[n], device_id={"theta": partner}, device_id_type=MESH,
+        ).start()
+
+    mine = pl.ds(pl.multiple_of(my_o * 8, 8), 8)
+
+    def work(n):
+        @pl.when(helper & (n == 0))
         def _():
             keep_copy.wait_recv()
 
-        mine = pl.ds(pl.multiple_of(my_o * 8, 8), 8)
-        which = jnp.where(helper, 1, 0)
-        kept_rows = keep[which, mine, :]
+        kept_rows = keep[jnp.where(helper, 1, 0), mine, :]
         kept_rows = jnp.concatenate([kept_rows, kept_rows], axis=1)
         polar = jnp.maximum(tab[4, mine, :], jnp.where(helper, F32(1.0), F32(0.0)))
         polar = jnp.concatenate([polar, polar], axis=1) > 0.5
-
-        def work(n, _):
-            pltpu.make_async_copy(rx.at[n], rx.at[n], a_recv.at[n]).wait()
-            blocks = [rx[n, p].reshape(24, 256) for p in range(PHI)]
-            done = filter_lines(blocks, kept_rows, modes, fwd, inv, one, back)
-            for p in range(PHI):
-                yb[n, p] = jnp.where(polar[None], done[p].reshape(3, 8, 256), rx[n, p])
-
+        pltpu.make_async_copy(rx.at[n], rx.at[n], a_recv.at[n]).wait()
+        blocks = [rx[n, p].reshape(24, 256) for p in range(PHI)]
+        done = filter_lines(blocks, kept_rows, modes, fwd, inv, one, back)
+        for p in range(PHI):
+            yb[n, p] = jnp.where(polar[None], done[p].reshape(3, 8, 256), rx[n, p])
+
+        @pl.when(source)
+        def _():
+            pltpu.make_async_copy(
+                yb.at[n, phi],
+                res.at[pl.ds(3 * n, 3), my_i, pl.ds(pl.multiple_of(my_o * 8, 8), 8), :],
+                b_recv.at[n],
+            ).start()
             for k in range(1, PHI):
                 b_copy(n, others(k)).start()
 
-            @pl.when(helper)
-            def _():
-                b_copy(n, phi).start()
-
-            @pl.when(source)
-            def _():
-                pltpu.make_async_copy(
-                    yb.at[n, phi],
-                    res.at[pl.ds(3 * n, 3), my_i, pl.ds(pl.multiple_of(my_o * 8, 8), 8), :],
-                    b_recv.at[n],
-                ).start()
-
-            return 0
-
-        lax.fori_loop(0, STAGES, work, 0)
+        @pl.when(helper)
+        def _():
+            pltpu.make_async_copy(yb.at[n, phi], rel.at[n, :, my_i, relay_rows, :], rel_recv.at[n]).start()
+            for k in range(1, PHI):
+                gather_copy(n, others(k)).start()
 
     acc[...] = jnp.zeros((32, 128), F32)
     lane = lax.broadcasted_iota(jnp.int32, (32, 128), 1)
@@ -408,7 +428,7 @@
     def out_copy(n):
         return pltpu.make_async_copy(res.at[pl.ds(3 * n, 3)], out.at[pl.ds(3 * n, 3)], out_sem.at[n])
 
-    def finish(n, _):
+    def finish(n):
         @pl.when(heavy)
         def _():
             whole = res.at[pl.ds(3 * n, 3)]
@@ -429,9 +449,29 @@
                 summed = jnp.sum(terms[c][:, :128] + terms[c][:, 128:], axis=1, keepdims=True)
                 total = jnp.where(lane == 4 * (3 * n + c) + i, jnp.broadcast_to(summed, (32, 128)), total)
         acc[...] = total
+
+    def tick(t, _):
+        @pl.when(t < STAGES)
+        def _():
+            step(t)
+
+        now = jnp.where(helper, t - HELP, t - BEHIND)
+
+        @pl.when(worker & (now >= 0) & (now < STAGES))
+        def _():
+            work(now)
+
+        @pl.when(helper & (now >= 1) & (now <= STAGES))
+        def _():
+            relay(now - 1)
+
+        @pl.when(t >= LAG)
+        def _():
+            finish(t - LAG)
+
         return 0
 
-    lax.fori_loop(0, STAGES, finish, 0)
+    lax.fori_loop(0, STAGES + LAG, tick, 0)
 
     def emf_copy(k):
         p = others(k)
@@ -449,12 +489,8 @@
     summed = summed * (1.0 / NPHI)
     emf[...] = jnp.where(phi % 2 == 0, summed[:4], summed[4:])
 
-    def drain(ref, sem):
-        pltpu.make_async_copy(ref, ref, sem).wait()
-
     seven = got.at[pl.ds(0, 7)]
     drain(seven, emf_send)
-    drain(halo_r, row_send)
 
     @pl.when(theta > 0)
     def _():
@@ -467,16 +503,20 @@
     @pl.when(heavy)
     def _():
         keep_copy.wait_send()
-        drain(rx, a_send.at[1])
+        for n in range(ACROSS):
+            drain(rx.at[0], across_send.at[n])
 
     @pl.when(source)
     def _():
-        drain(rx.at[:, pl.ds(0, 7)], a_send.at[0])
+        drain(rx.at[:, pl.ds(0, 7)], a_send)
+
+    @pl.when(worker)
+    def _():
         drain(yb.at[:, pl.ds(0, 7)], b_send)
 
     @pl.when(helper)
     def _():
-        drain(yb, b_send)
+        drain(rel, rel_send)
 
     def drain_out(n, _):
         out_copy(n).wait()
@@ -488,9 +528,8 @@
 def body(test_fields, velocity, kept):
     forward, inverse, singles, singles_back, modes = fourier_constants()
     tables = row_tables()
-    hbm, vmem = pl.BlockSpec(memory_space=pl.ANY), pl.BlockSpec(memory_space=pltpu.VMEM)
-    dma, regular = pltpu.SemaphoreType.DMA, pltpu.SemaphoreType.REGULAR
-    del regular
+    hbm, vmem = pl.BlockSpec(memory_space=pltpu.HBM), pl.BlockSpec(memory_space=pltpu.VMEM)
+    dma = pltpu.SemaphoreType.DMA
     result, emf = pl.pallas_call(
         kernel,
         out_shape=(
@@ -517,25 +556,29 @@
             pltpu.VMEM((STAGES, PHI, 3, 8, 256), F32),
             pltpu.VMEM((STAGES, PHI, 3, 8, 256), F32),
             pltpu.VMEM((27, 4, 32, 256), F32),
+            pltpu.VMEM((STAGES, 3, 4, 16, 256), F32),
             pltpu.VMEM((32, 128), F32),
             pltpu.VMEM((PHI, 8, 128), F32),
             dma((8,)),
             dma((2,)),
             dma((2,)),
-            dma,
-            dma((STAGES,)),
-            dma,
-            dma,
-            dma((2,)),
-            dma((STAGES,)),
-            dma,
             dma((STAGES,)),
             dma((STAGES,)),
             dma,
             dma,
+            dma,
+            dma((ACROSS,)),
+            dma((STAGES,)),
+            dma,
+            dma((STAGES,)),
+            dma,
+            dma((STAGES,)),
+            dma((STAGES,)),
+            dma,
+            dma,
         ],
         compiler_params=pltpu.CompilerParams(
-            collective_id=0, has_side_effects=True, vmem_limit_bytes=48 * 2**20
+            collective_id=0, has_side_effects=True, vmem_limit_bytes=62 * 2**20
         ),
         name="substep",
     )(

time: 94.3 us -> 82.9 us (0.88)
  local copies, waits for them, and re-layouts: 13.3 us -> 5.75 us
  Pallas kernels: 79.9 us -> 76.4 us
    unnamed x18 -> x2, local copies, waits for them, and re-layouts: 13.2 us -> 4.97 us
    pallas_call x1, Pallas kernels: 79.9 us -> 76.4 us  [body(): pl.pallas_call(kernel, out_shape=(jax.ShapeDtypeStruct((27, 4, 32, 256),...]
where the time goes in v2:
time: 82.9 us; the launch traced here: 82.8 us
  Pallas kernels  76.4 us (92%)
  local copies, waits for them, and re-layouts  5.75 us (7%)
    pallas_call x1, Pallas kernels, body(): pl.pallas_call(kernel, out_shape=(jax.ShapeDtypeStruct((27, 4, 32, 256),...  76.4 us
    unnamed x2, local copies, waits for them, and re-layouts  4.97 us

profile of v2, /device:TPU:1, one launch (start us, length us, event | category | flops | bytes accessed | tf_op | source)
XLA Modules:
  0.0 82.8 jit_solution(12694465958135938061)
XLA Ops:
  0.6 76.4 %substep.1 = (f32[27,4,32,256]{3,2,1,0:T(8,128)}, f32[4,128]{1,0:T(4,128)}) custom-call(f32[27,4,32,256]{3,2,1,0:T(8,128)} %tf.1, f32[3,4,32,256]{3,2,1,0:T(8,128)} %vel.1, s32[1,32]{1,0:T(1,128)} %bitcast.5, f32[8,5,32,128]{3,2,1,0:T(8,128)} %constant.12.clone.tab_hbm, bf16[2,3,512,256]{3,2,1,0:T(8,128)(2,1)} %constant.13.clone.fwd_hbm, ...), custom_call_target="tpu_custom_call" | custom-call | tf_op jit(solution)/shard_map/substep/pallas_call | solution.py:533
  77.0 0.7 slice_bitcast_fusion
  77.7 0.1 reshape.11
  77.8 0.7 copy.12
  78.5 4.3 %copy.14 = f32[27,4,32,256]{3,2,1,0:T(8,128)} copy(f32[27,4,32,256]{3,2,1,0:T(8,128)} %get-tuple-element.12) | data formatting | bytes 7077888

commit v3 on v2

v3 whole, which is shorter than its diff:
```python
import functools
import math

import jax
import jax.numpy as jnp
import ml_dtypes
import numpy as np
from jax import lax
from jax.experimental import pallas as pl
from jax.experimental.pallas import tpu as pltpu
from jax.sharding import PartitionSpec as P

MESH = pl.DeviceIdType.MESH
NPHI = 2048
MMAX = 512
STAGES = 9
AHEAD = 3
ELAG = 1
PIECES = ((0, 1), (1, 4), (4, 9))
ACROSS = 2
LAG = 12
BEHIND = 4
LIGHT_BEHIND = 4
HELP = 0
FAR = 0
VIA = 2
PLAN = ("FH", "OF", "OH", "FH", "OF", "OH", "OF", "OH", "OH")
FAR_WORK = (("L", 0), ("H", 0), ("H", 1), ("H", 3), ("H", 4), ("H", 6))
OWN = tuple(n for n in range(STAGES) if "O" in PLAN[n])
HELPED = tuple(n for n in range(STAGES) if "H" in PLAN[n])
FARRED = tuple(n for n in range(STAGES) if "F" in PLAN[n])
LIGHT_FAR = tuple(n for kind, n in FAR_WORK if kind == "L")
LIGHT_OWN = tuple(n for n in range(STAGES) if n not in LIGHT_FAR)
PHI = 8
F32 = jnp.float32
BF16 = jnp.bfloat16


def split_bf16(a):
    hi = a.astype(ml_dtypes.bfloat16)
    lo = (a - hi.astype(np.float64)).astype(ml_dtypes.bfloat16)
    return np.stack([hi, lo])


def fourier_constants():
    cell = np.arange(256)
    block = np.arange(64)

    def tables(mode):
        angle = 2.0 * math.pi * ((cell[:, None] * mode[None, :]) % NPHI) / NPHI
        return np.cos(angle), np.sin(angle)

    def scale(mode):
        return np.where(mode == 0, 1.0 / NPHI, 2.0 / NPHI)

    forward, inverse, modes = [], [], []
    singles, singles_back = [], []
    for r in (0, 4):
        mode = 8 * block + r
        c, s = tables(mode)
        full = np.concatenate([c, s], axis=1)
        singles.append(full)
        singles_back.append((full * np.tile(scale(mode), 2)).T)
        modes.append(np.tile(mode, 2))
    modes = [np.concatenate(modes)]
    for r in (1, 2, 3):
        m, n = 8 * block + r, 8 * block + 8 - r
        cm, sm = tables(m)
        cn, sn = tables(n)
        upper = np.concatenate([cm, sm, cn, sn], axis=1)
        lower = np.concatenate([-sm, cm, sn, -cn], axis=1)
        full = np.concatenate([upper, lower], axis=0)
        weights = np.concatenate([scale(m), scale(m), scale(n), scale(n)])
        forward.append(full)
        inverse.append((full * weights).T)
        modes.append(np.concatenate([m, m, n, n]))
    modes = np.broadcast_to(np.stack(modes).astype(np.float32)[:, None, :], (4, 8, 256))
    return (
        split_bf16(np.stack(forward)),
        split_bf16(np.stack(inverse)),
        split_bf16(np.stack(singles)),
        split_bf16(np.stack(singles_back)),
        np.ascontiguousarray(modes),
    )


def row_tables():
    j = np.arange(256)
    d = math.pi / 256
    angle = d * (j + 0.5)
    south = np.sin(angle + 0.5 * d) / np.sin(angle)
    north = np.sin(angle - 0.5 * d) / np.sin(angle)
    polar = (3 * (2 * j + 1) < 256) | (3 * (2 * (255 - j) + 1) < 256)
    kinds = np.stack([south, north, np.cos(angle), np.sin(angle), polar.astype(np.float64)])
    kinds = kinds.reshape(5, 8, 32).transpose(1, 0, 2)
    return np.ascontiguousarray(np.broadcast_to(kinds[..., None], (8, 5, 32, 128)).astype(np.float32))


def radial_constants():
    h = 0.3 / 8
    r = 0.7 + h * (np.arange(8) + 0.5)
    return ((r + h / 2) / r) ** 2, ((r - h / 2) / r) ** 2, (1.0 / r) ** 2


def split_rows(a):
    hi = a.astype(BF16).astype(F32)
    return jnp.concatenate([hi, a - hi], axis=0).astype(BF16)


def dot(a, b):
    return jnp.dot(a, b, preferred_element_type=F32)


def dot_split(a, high, low):
    lines = a.shape[0]
    both = split_rows(a)
    out = dot(both, high) + dot(both, low)
    return out[:lines] + out[lines:]


def filter_lines(blocks, keep, modes, fwd, inv, one, back):
    x0, x1, x2, x3, x4, x5, x6, x7 = blocks
    half = math.sqrt(0.5)
    s04, d04, s26, d26 = x0 + x4, x0 - x4, x2 + x6, x2 - x6
    s15, d15, s37, d37 = x1 + x5, x1 - x5, x3 + x7, x3 - x7
    even, odd = s04 + s26, s15 + s37
    cross, plus = half * (d15 - d37), half * (d15 + d37)
    pairs = [(d04 + cross, d26 + plus), (s04 - s26, s15 - s37), (d04 - cross, plus - d26)]

    def masked(mid, group):
        lines = mid.shape[0]
        kept = mid.reshape(lines // 8, 8, 256)
        kept = jnp.where((modes[group] < keep)[None], kept, 0.0)
        return kept.reshape(lines, 256)

    mid = jnp.concatenate(
        [dot_split(even + odd, one[0, 0], one[1, 0]), dot_split(even - odd, one[0, 1], one[1, 1])], axis=1
    )
    mid = masked(mid, 0)
    p0 = dot_split(mid[:, :128], back[0, 0], back[1, 0])
    p4 = dot_split(mid[:, 128:], back[0, 1], back[1, 1])
    p, q = [], []
    for r, (u, v) in enumerate(pairs):
        mid = dot_split(jnp.concatenate([u, v], axis=1), fwd[0, r], fwd[1, r])
        mid = masked(mid, r + 1)
        out = dot_split(mid, inv[0, r], inv[1, r])
        p.append(out[:, :256])
        q.append(out[:, 256:])
    (p1, p2, p3), (q1, q2, q3) = p, q
    a, b = p0 + p4, p0 - p4
    p13, q13 = p1 + p3, q1 - q3
    ph, qh = half * (p1 - p3), half * (q1 + q3)
    ap, am, bp, bm = a + p2, a - p2, b + q2, b - q2
    return [
        ap + p13,
        bp + (ph + qh),
        am + q13,
        bm - (ph - qh),
        ap - p13,
        bp - (ph + qh),
        am - q13,
        bm + (ph - qh),
    ]


def member(n, values):
    found = n == values[0]
    for value in values[1:]:
        found = found | (n == value)
    return found


def rank(n, values):
    return sum(jnp.where(n > value, 1, 0) for value in values)


def pick(n, values):
    out = values[0]
    for k in range(1, len(values)):
        out = jnp.where(n >= k, values[k], out)
    return out


def kernel(
    tf, vel, kept_hbm, tab_hbm, fwd_hbm, inv_hbm, one_hbm, back_hbm, modes_hbm,
    res, emf,
    xp, v, kept, tab, fwd, inv, one, back, modes,
    edge, halo_t, halo_r, coef, radius, keep, mask, st, rx, yb, rel, vb, acc, got,
    load_sem, theta_send, theta_recv, row_send, row_recv, keep_send, keep_recv,
    a_send, across_send, via_send, via_recv, far_send, a_recv, b_send, b_recv, rel_send, rel_recv, emf_send, emf_recv,
):
    phi, theta, row = lax.axis_index("phi"), lax.axis_index("theta"), lax.axis_index("row")
    group = theta % 2
    heavy_at, helper_at, far_at, light_at = 7 * group, 2 + 3 * group, 4 - group, 6 - 5 * group
    heavy, helper, far, light = theta == heavy_at, theta == helper_at, theta == far_at, theta == light_at
    source = heavy | light
    light_octet = 2 - 2 * group
    octet = jnp.where(light, light_octet, 0)
    my_i, my_half = phi // 2, phi % 2
    edge_i, main_i = 3 - 3 * row, row
    late = jnp.where(my_i == edge_i, ELAG, 0)

    def others(k):
        return lax.rem(phi + k, PHI)

    loads = [
        pltpu.make_async_copy(tf, xp.at[:, :, pl.ds(8, 32), :], load_sem.at[0]),
        pltpu.make_async_copy(vel, v, load_sem.at[1]),
        pltpu.make_async_copy(tab_hbm.at[theta], tab, load_sem.at[2]),
        pltpu.make_async_copy(fwd_hbm, fwd, load_sem.at[3]),
        pltpu.make_async_copy(inv_hbm, inv, load_sem.at[4]),
        pltpu.make_async_copy(one_hbm, one, load_sem.at[5]),
        pltpu.make_async_copy(back_hbm, back, load_sem.at[6]),
        pltpu.make_async_copy(modes_hbm, modes, load_sem.at[7]),
        pltpu.make_async_copy(tab_hbm.at[jnp.where(far, light_at, theta), 4], mask, load_sem.at[8]),
        pltpu.make_async_copy(kept_hbm, kept, load_sem.at[9]),
    ]
    for load in loads:
        load.start()

    barrier = pltpu.get_barrier_semaphore()
    pl.semaphore_signal(barrier, inc=1, device_id={"row": 1 - row}, device_id_type=MESH)
    for k in range(1, PHI):
        pl.semaphore_signal(barrier, inc=1, device_id={"phi": others(k)}, device_id_type=MESH)

    @pl.when(theta > 0)
    def _():
        pl.semaphore_signal(barrier, inc=1, device_id={"theta": theta - 1}, device_id_type=MESH)

    @pl.when(theta < 7)
    def _():
        pl.semaphore_signal(barrier, inc=1, device_id={"theta": theta + 1}, device_id_type=MESH)

    def greet_all(there):
        for k in range(PHI):
            pl.semaphore_signal(barrier, inc=1, device_id={"theta": there, "phi": others(k)}, device_id_type=MESH)

    def greet(there):
        pl.semaphore_signal(barrier, inc=1, device_id={"theta": there}, device_id_type=MESH)

    @pl.when(heavy)
    def _():
        greet_all(helper_at)
        greet(far_at)
        greet(light_at)

    @pl.when(helper)
    def _():
        greet_all(heavy_at)

    @pl.when(far)
    def _():
        greet_all(light_at)
        greet(heavy_at)

    @pl.when(light)
    def _():
        greet_all(far_at)
        greet(heavy_at)

    loads[0].wait()

    def pack(f, _):
        for i in range(4):
            edge[0, f, pl.ds(i, 1), :] = xp[f, i, pl.ds(8, 1), :]
            edge[1, f, pl.ds(i, 1), :] = xp[f, i, pl.ds(39, 1), :]
        return 0

    lax.fori_loop(0, 27, pack, 0)
    loads[9].wait()
    eye = lax.broadcasted_iota(jnp.int32, (32, 32), 0) == lax.broadcasted_iota(jnp.int32, (32, 32), 1)
    counts = jnp.where(eye, jnp.broadcast_to(kept[...], (32, 32)), 0).astype(F32)
    keep[0] = jnp.broadcast_to(jnp.sum(counts, axis=1, keepdims=True), (32, 128))

    peers = PHI + jnp.where(theta > 0, 1, 0) + jnp.where(theta < 7, 1, 0) + PHI
    peers = peers + jnp.where(heavy, 2, 0) + jnp.where(far | light, 1, 0)
    pl.semaphore_wait(barrier, peers)

    def theta_copy(n, side, there):
        first, last = PIECES[n]
        part = pl.ds(3 * first, 3 * (last - first))
        return pltpu.make_async_remote_copy(
            src_ref=edge.at[side, part], dst_ref=halo_t.at[side, part], send_sem=theta_send.at[side, n],
            recv_sem=theta_recv.at[side, n], device_id={"theta": there}, device_id_type=MESH)


    def row_copy(n):
        return pltpu.make_async_remote_copy(
            src_ref=xp.at[pl.ds(3 * n, 3), edge_i, pl.ds(8, 32), :], dst_ref=halo_r.at[pl.ds(3 * n, 3)],
            send_sem=row_send.at[n], recv_sem=row_recv.at[n],
            device_id={"row": 1 - row}, device_id_type=MESH)

    def send_theta(n):
        @pl.when(theta > 0)
        def _():
            theta_copy(n, 0, theta - 1).start()

        @pl.when(theta < 7)
        def _():
            theta_copy(n, 1, theta + 1).start()

    def wait_theta(n):
        @pl.when(theta > 0)
        def _():
            theta_copy(n, 0, theta).wait_send()
            theta_copy(n, 1, theta).wait_recv()

        @pl.when(theta < 7)
        def _():
            theta_copy(n, 1, theta).wait_send()
            theta_copy(n, 0, theta).wait_recv()

    send_theta(0)
    row_copy(0).start()
    send_theta(1)
    for n in range(1, AHEAD):
        row_copy(n).start()

    def keep_copy(slot, sem, there):
        return pltpu.make_async_remote_copy(
            src_ref=keep.at[0], dst_ref=keep.at[slot], send_sem=keep_send.at[sem], recv_sem=keep_recv.at[slot - 1],
            device_id={"theta": there}, device_id_type=MESH)

    @pl.when(heavy)
    def _():
        keep_copy(1, 0, helper_at).start()
        keep_copy(1, 1, far_at).start()

    @pl.when(light)
    def _():
        keep_copy(2, 0, far_at).start()

    for load in loads[1:9]:
        load.wait()
    outward, inward, metric = radial_constants()

    def radial(values, i):
        return jnp.where(row == 0, F32(values[i]), F32(values[i + 4]))

    for i in range(4):
        radius[0, i] = 0.2 * radial(outward, i) * (1.0 if i < 3 else jnp.where(row == 0, F32(1.0), F32(0.0)))
        radius[1, i] = 0.2 * radial(inward, i) * (1.0 if i > 0 else jnp.where(row == 1, F32(1.0), F32(0.0)))

    south, north = tab[0], tab[1]
    for i in range(4):
        g = 0.1 * radial(metric, i)
        cs, cn = g * south, g * north
        both = 0.2 * (radial(outward, i) + radial(inward, i))
        centre = (1.0 - both) - (cs + cn)
        for lanes in range(2):
            part = pl.ds(128 * lanes, 128)
            coef[0, i, :, part] = cs
            coef[1, i, :, part] = cn
            coef[2, i, :, part] = centre

    @pl.when(theta == 7)
    def _():
        halo_t[0] = jnp.zeros((27, 4, 256), F32)

    @pl.when(theta == 0)
    def _():
        halo_t[1] = jnp.zeros((27, 4, 256), F32)

    def drain(ref, sem):
        pltpu.make_async_copy(ref, ref, sem).wait()

    def chunk(n, p, rows):
        return st.at[pl.ds(3 * n, 3), p // 2, pl.ds(pl.multiple_of((rows + p % 2) * 8, 8), 8), :]

    def a_copy(n, p, there, rows, slot, sem):
        return pltpu.make_async_remote_copy(
            src_ref=chunk(n, p, rows), dst_ref=rx.at[slot, phi], send_sem=sem, recv_sem=a_recv.at[slot],
            device_id={"theta": there, "phi": p}, device_id_type=MESH)

    main_workers = [2 * main_i + lax.rem(phi + q, 6) for q in range(6)]
    edge_workers = [2 * edge_i + lax.rem(phi + q, 2) for q in range(2)]

    def far_octet(n):
        return jnp.where(member(n, OWN), 2, 0)

    def via_copy(n, part):
        r = rank(n, FARRED)
        layers = pl.ds(main_i, 3) if part == 0 else pl.ds(edge_i, 1)
        return pltpu.make_async_remote_copy(
            src_ref=st.at[pl.ds(3 * n, 3), layers, pl.ds(pl.multiple_of(far_octet(n) * 8, 8), 16), :],
            dst_ref=vb.at[r, :, layers], send_sem=via_send.at[part, lax.rem(r, ACROSS)],
            recv_sem=via_recv.at[part, r], device_id={"theta": light_at}, device_id_type=MESH)

    def pass_on(r, part):
        got_part = vb.at[r, :, pl.ds(main_i, 3)] if part == 0 else vb.at[r, :, pl.ds(edge_i, 1)]
        pltpu.make_async_copy(got_part, got_part, via_recv.at[part, r]).wait()
        slot = pick(r, [k for k, (kind, _) in enumerate(FAR_WORK) if kind == "H"])
        for p in main_workers if part == 0 else edge_workers:
            pltpu.make_async_remote_copy(
                src_ref=vb.at[r, :, p // 2, pl.ds(pl.multiple_of(p % 2 * 8, 8), 8), :],
                dst_ref=rx.at[slot, phi], send_sem=far_send, recv_sem=a_recv.at[slot],
                device_id={"theta": far_at, "phi": p}, device_id_type=MESH,
            ).start()

    def layer(n, i, neighbours):
        p_unit, q_unit = n // 3, n % 3
        unit = [jnp.where(p_unit == k, F32(0.5), F32(0.0)) for k in range(3)]
        weight = [jnp.where(q_unit == k, F32(1.0), F32(0.0)) for k in range(3)]
        profile = weight[0] + weight[1] * tab[2] + weight[2] * tab[3]
        profile = jnp.concatenate([profile, profile], axis=1)
        v0, v1, v2 = v[0, i], v[1, i], v[2, i]
        turned = (v1 * unit[2] - v2 * unit[1], v2 * unit[0] - v0 * unit[2], v0 * unit[1] - v1 * unit[0])
        for c in range(3):
            f = 3 * n + c
            xp[f, i, pl.ds(7, 1), :] = halo_t[1, f, pl.ds(i, 1), :]
            xp[f, i, pl.ds(40, 1), :] = halo_t[0, f, pl.ds(i, 1), :]
            total = coef[2, i] * xp[f, i, pl.ds(8, 32), :] + profile * turned[c]
            for factor, other in neighbours(f):
                total = total + factor * other
            total = total + coef[0, i] * xp[f, i, pl.ds(9, 32), :] + coef[1, i] * xp[f, i, pl.ds(7, 32), :]
            st[f, i] = total

        @pl.when(light)
        def _():
            rest = pl.ds(pl.multiple_of(16 - 8 * light_octet, 8), 16)
            for c in range(3):
                res[3 * n + c, i, rest, :] = st[3 * n + c, i, rest, :]

        @pl.when(jnp.logical_not(source))
        def _():
            for c in range(3):
                res[3 * n + c, i] = st[3 * n + c, i]

    def send(n, part):
        workers = main_workers if part == 0 else edge_workers

        @pl.when((heavy & member(n, OWN)) | (light & member(n, LIGHT_OWN)))
        def _():
            for p in workers:

                @pl.when(p == phi)
                def _(p=p):
                    pltpu.make_async_copy(chunk(n, p, octet), rx.at[n, phi], a_recv.at[n]).start()

                @pl.when(p != phi)
                def _(p=p):
                    a_copy(n, p, theta, octet, n, a_send).start()

        @pl.when(light & member(n, LIGHT_FAR))
        def _():
            slot = pick(rank(n, LIGHT_FAR), [k for k, (kind, _) in enumerate(FAR_WORK) if kind == "L"])
            for p in workers:
                a_copy(n, p, far_at, octet, slot, far_send).start()

        @pl.when(heavy & member(n, FARRED))
        def _():
            @pl.when(rank(n, FARRED) >= ACROSS)
            def _():
                via_copy(n, part).wait_send()

            via_copy(n, part).start()

        @pl.when(heavy & member(n, HELPED))
        def _():
            r = rank(n, HELPED)
            sem = across_send.at[part, lax.rem(r, ACROSS)]

            @pl.when(r >= ACROSS)
            def _():
                drain(rx.at[0, pl.ds(0, len(workers))], sem)

            for p in workers:
                a_copy(n, p, helper_at, 2, n, sem).start()

    def step_main(n):
        for k, (first, _) in enumerate(PIECES):

            @pl.when(n == first)
            def _(k=k):
                wait_theta(k)

        @pl.when(n == 0)
        def _():
            send_theta(2)

        for m in range(3):
            i = main_i + m

            def neighbours(f, i=i):
                up, down = jnp.minimum(i + 1, 3), jnp.maximum(i - 1, 0)
                return (
                    (radius[0, i], xp[f, up, pl.ds(8, 32), :]),
                    (radius[1, i], xp[f, down, pl.ds(8, 32), :]),
                )

            layer(n, i, neighbours)
        send(n, 0)

    def step_edge(n):
        row_copy(n).wait_recv()
        row_copy(n).wait_send()

        @pl.when(n + AHEAD < STAGES)
        def _():
            row_copy(n + AHEAD).start()

        def neighbours(f):
            return (
                (radius[row, edge_i], halo_r[f]),
                (radius[1 - row, edge_i], xp[f, 2 - row, pl.ds(8, 32), :]),
            )

        layer(n, edge_i, neighbours)
        send(n, 1)

    half_rows = pl.ds(pl.multiple_of(my_half * 8, 8), 8)

    def b_copy(n, p):
        return pltpu.make_async_remote_copy(
            src_ref=yb.at[n, p],
            dst_ref=res.at[pl.ds(3 * n, 3), my_i, pl.ds(pl.multiple_of((octet + my_half) * 8, 8), 8), :],
            send_sem=b_send, recv_sem=b_recv.at[n],
            device_id={"phi": p}, device_id_type=MESH)

    def gather_copy(slot, p):
        return pltpu.make_async_remote_copy(
            src_ref=yb.at[slot, p], dst_ref=rel.at[slot, :, my_i, half_rows, :],
            send_sem=b_send, recv_sem=rel_recv.at[slot], device_id={"phi": p}, device_id_type=MESH)

    far_light = [1 if kind == "L" else 0 for kind, _ in FAR_WORK]
    far_stage = [n for _, n in FAR_WORK]

    def relay(slot):
        pltpu.make_async_copy(rel.at[slot], rel.at[slot], rel_recv.at[slot]).wait()
        to_light = far & (pick(slot, far_light) == 1)
        n = jnp.where(far, pick(slot, far_stage), slot)
        rows = jnp.where(to_light, light_octet, jnp.where(far, far_octet(n), 2))
        pltpu.make_async_remote_copy(
            src_ref=rel.at[slot],
            dst_ref=res.at[pl.ds(3 * n, 3), :, pl.ds(pl.multiple_of(rows * 8, 8), 16), :],
            send_sem=rel_send, recv_sem=b_recv.at[n],
            device_id={"theta": jnp.where(to_light, light_at, heavy_at)}, device_id_type=MESH,
        ).start()

    def work(slot):
        @pl.when((helper & (slot == HELPED[0])) | (far & (slot == 0)))
        def _():
            keep_copy(1, 0, theta).wait_recv()

        @pl.when(far & (slot == 0))
        def _():
            keep_copy(2, 0, theta).wait_recv()

        on_light = far & (pick(slot, far_light) == 1)
        far_rows = jnp.where(on_light, light_octet, far_octet(pick(slot, far_stage)))
        rows = jnp.where(far, far_rows, jnp.where(helper, 2, octet)) + my_half
        mine = pl.ds(pl.multiple_of(rows * 8, 8), 8)
        kept_rows = keep[jnp.where(on_light, 2, jnp.where(source, 0, 1)), mine, :]
        kept_rows = jnp.concatenate([kept_rows, kept_rows], axis=1)
        polar = jnp.maximum(mask[mine, :], jnp.where(light | on_light, F32(0.0), F32(1.0)))
        polar = jnp.concatenate([polar, polar], axis=1) > 0.5
        pltpu.make_async_copy(rx.at[slot], rx.at[slot], a_recv.at[slot]).wait()
        blocks = [rx[slot, p].reshape(24, 256) for p in range(PHI)]
        done = filter_lines(blocks, kept_rows, modes, fwd, inv, one, back)
        for p in range(PHI):
            yb[slot, p] = jnp.where(polar[None], done[p].reshape(3, 8, 256), rx[slot, p])

        @pl.when(source)
        def _():
            pltpu.make_async_copy(
                yb.at[slot, phi], res.at[pl.ds(3 * slot, 3), my_i, mine, :], b_recv.at[slot]
            ).start()
            for k in range(1, PHI):
                b_copy(slot, others(k)).start()

        @pl.when(jnp.logical_not(source))
        def _():
            pltpu.make_async_copy(
                yb.at[slot, phi], rel.at[slot, :, my_i, half_rows, :], rel_recv.at[slot]
            ).start()
            for k in range(1, PHI):
                gather_copy(slot, others(k)).start()

    acc[...] = jnp.zeros((32, 128), F32)
    lane = lax.broadcasted_iota(jnp.int32, (32, 128), 1)

    def finish(n):
        @pl.when(heavy)
        def _():
            whole = res.at[pl.ds(3 * n, 3)]
            pltpu.make_async_copy(whole, whole, b_recv.at[n]).wait()

        @pl.when(light)
        def _():
            part = res.at[pl.ds(3 * n, 3), :, pl.ds(pl.multiple_of(octet * 8, 8), 16), :]
            pltpu.make_async_copy(part, part, b_recv.at[n]).wait()

        total = acc[...]
        for i in range(4):
            v0, v1, v2 = v[0, i], v[1, i], v[2, i]
            r0, r1, r2 = res[3 * n, i], res[3 * n + 1, i], res[3 * n + 2, i]
            terms = (v1 * r2 - v2 * r1, v2 * r0 - v0 * r2, v0 * r1 - v1 * r0)
            for c in range(3):
                summed = jnp.sum(terms[c][:, :128] + terms[c][:, 128:], axis=1, keepdims=True)
                total = jnp.where(lane == 27 * i + 3 * n + c, jnp.broadcast_to(summed, (32, 128)), total)
        acc[...] = total

    def tick(t, _):
        @pl.when(t < STAGES)
        def _():
            step_main(t)

        @pl.when((t >= ELAG) & (t < STAGES + ELAG))
        def _():
            step_edge(t - ELAG)

        for part in range(2):
            first = VIA + ELAG * part

            @pl.when(light & (t >= first) & (t < first + len(FARRED)))
            def _(part=part, first=first):
                pass_on(t - first, part)

        def busy(slot):
            mine = (heavy & member(slot, OWN)) | (light & member(slot, LIGHT_OWN))
            theirs = (helper & member(slot, HELPED)) | (far & (slot >= 0) & (slot < len(FAR_WORK)))
            return mine | theirs

        at = t - jnp.where(helper, HELP, jnp.where(far, FAR, jnp.where(light, LIGHT_BEHIND, BEHIND)))

        @pl.when(busy(at - late))
        def _():
            work(at - late)

        @pl.when((helper | far) & busy(at - ELAG - 1))
        def _():
            relay(at - ELAG - 1)

        @pl.when(t >= LAG)
        def _():
            finish(t - LAG)

        return 0

    lax.fori_loop(0, STAGES + LAG, tick, 0)

    def emf_copy(k):
        p = others(k)
        return pltpu.make_async_remote_copy(
            src_ref=acc.at[pl.ds(pl.multiple_of(p // 2 * 8, 8), 8), :], dst_ref=got.at[phi],
            send_sem=emf_send, recv_sem=emf_recv, device_id={"phi": p}, device_id_type=MESH)

    for k in range(1, PHI):
        emf_copy(k).start()
    pltpu.make_async_copy(acc.at[pl.ds(pl.multiple_of(phi // 2 * 8, 8), 8), :], got.at[phi], emf_recv).start()
    pltpu.make_async_copy(got, got, emf_recv).wait()
    summed = got[0]
    for p in range(1, PHI):
        summed = summed + got[p]
    summed = summed * (1.0 / NPHI)
    mean = jnp.where(phi % 2 == 0, summed[:4], summed[4:])
    for i in range(4):
        emf[i] = mean[:, 27 * i : 27 * i + 27]

    seven = got.at[pl.ds(0, 7)]
    drain(seven, emf_send)

    @pl.when(heavy)
    def _():
        keep_copy(1, 0, theta).wait_send()
        keep_copy(1, 1, theta).wait_send()
        for n in range(ACROSS):
            drain(rx.at[0, pl.ds(0, 6)], across_send.at[0, n])
            drain(rx.at[0, pl.ds(0, 2)], across_send.at[1, n])
            drain(vb.at[0, :, pl.ds(0, 3)], via_send.at[0, n])
            drain(vb.at[0, :, pl.ds(0, 1)], via_send.at[1, n])
        drain(rx.at[pl.ds(0, len(OWN)), pl.ds(0, 7)], a_send)
        drain(yb.at[pl.ds(0, len(OWN)), pl.ds(0, 7)], b_send)

    @pl.when(light)
    def _():
        keep_copy(2, 0, theta).wait_send()
        drain(rx.at[pl.ds(0, len(LIGHT_OWN)), pl.ds(0, 7)], a_send)
        drain(yb.at[pl.ds(0, len(LIGHT_OWN)), pl.ds(0, 7)], b_send)
        drain(rx.at[pl.ds(0, len(FAR_WORK))], far_send)

    @pl.when(helper)
    def _():
        drain(yb.at[pl.ds(0, len(HELPED)), pl.ds(0, 7)], b_send)
        drain(rel.at[pl.ds(0, len(HELPED))], rel_send)

    @pl.when(far)
    def _():
        drain(yb.at[pl.ds(0, len(FAR_WORK)), pl.ds(0, 7)], b_send)
        drain(rel.at[pl.ds(0, len(FAR_WORK))], rel_send)


def body(test_fields, velocity, kept):
    forward, inverse, singles, singles_back, modes = fourier_constants()
    tables = row_tables()
    hbm, vmem = pl.BlockSpec(memory_space=pltpu.HBM), pl.BlockSpec(memory_space=pltpu.VMEM)
    dma = pltpu.SemaphoreType.DMA
    result, emf = pl.pallas_call(
        kernel,
        out_shape=(
            jax.ShapeDtypeStruct((27, 4, 32, 256), F32),
            jax.ShapeDtypeStruct((4, 4, 27), F32),
        ),
        in_specs=[hbm] * 9,
        out_specs=(vmem, vmem),
        scratch_shapes=[
            pltpu.VMEM((27, 4, 48, 256), F32),
            pltpu.VMEM((3, 4, 32, 256), F32),
            pltpu.VMEM((1, 32), jnp.int32),
            pltpu.VMEM((5, 32, 128), F32),
            pltpu.VMEM(forward.shape, BF16),
            pltpu.VMEM(inverse.shape, BF16),
            pltpu.VMEM(singles.shape, BF16),
            pltpu.VMEM(singles_back.shape, BF16),
            pltpu.VMEM(modes.shape, F32),
            pltpu.VMEM((2, 27, 4, 256), F32),
            pltpu.VMEM((2, 27, 4, 256), F32),
            pltpu.VMEM((27, 32, 256), F32),
            pltpu.VMEM((3, 4, 32, 256), F32),
            pltpu.SMEM((2, 4), F32),
            pltpu.VMEM((3, 32, 128), F32),
            pltpu.VMEM((32, 128), F32),
            pltpu.VMEM((27, 4, 32, 256), F32),
            pltpu.VMEM((STAGES, PHI, 3, 8, 256), F32),
            pltpu.VMEM((STAGES, PHI, 3, 8, 256), F32),
            pltpu.VMEM((STAGES, 3, 4, 16, 256), F32),
            pltpu.VMEM((len(FARRED), 3, 4, 16, 256), F32),
            pltpu.VMEM((32, 128), F32),
            pltpu.VMEM((PHI, 8, 128), F32),
            dma((10,)),
            dma((2, len(PIECES))),
            dma((2, len(PIECES))),
            dma((STAGES,)),
            dma((STAGES,)),
            dma((2,)),
            dma((2,)),
            dma,
            dma((2, ACROSS)),
            dma((2, ACROSS)),
            dma((2, len(FARRED))),
            dma,
            dma((STAGES,)),
            dma,
            dma((STAGES,)),
            dma,
            dma((STAGES,)),
            dma,
            dma,
        ],
        compiler_params=pltpu.CompilerParams(
            collective_id=0, has_side_effects=True, vmem_limit_bytes=40 * 2**20
        ),
        name="substep",
    )(
        *(
            pltpu.with_memory_space_constraint(jnp.asarray(a), pltpu.HBM)
            for a in (
                test_fields, velocity, kept.reshape(1, 32), tables, forward, inverse, singles, singles_back, modes,
            )
        )
    )
    return result, jnp.transpose(emf, (2, 0, 1))


def solution(mesh):
    return jax.shard_map(
        body,
        mesh=mesh,
        in_specs=(P(None, "row", "theta", "phi"), P(None, "row", "theta", "phi"), P("theta")),
        out_specs=(P(None, "row", "theta", "phi"), P(None, "row", ("theta", "phi"))),
        check_vma=False,
    )
```

time: 82.9 us -> 68.8 us (0.83)
  Pallas kernels: 76.4 us -> 65.2 us
  local copies, waits for them, and re-layouts: 5.75 us -> 2.39 us
    pallas_call x1, Pallas kernels: 76.4 us -> 65.2 us  [body(): pl.pallas_call(kernel, out_shape=(jax.ShapeDtypeStruct((27, 4, 32, 256),...]
    unnamed x2, local copies, waits for them, and re-layouts: 4.97 us -> 2.39 us
where the time goes in v3:
time: 68.8 us; the launch traced here: 68.2 us
  Pallas kernels  65.2 us (95%)
  local copies, waits for them, and re-layouts  2.39 us (3%)
    pallas_call x1, Pallas kernels, body(): pl.pallas_call(kernel, out_shape=(jax.ShapeDtypeStruct((27, 4, 32, 256),...  65.2 us
    unnamed x2, local copies, waits for them, and re-layouts  2.39 us

profile of v3, /device:TPU:1, one launch (start us, length us, event | category | flops | bytes accessed | tf_op | source)
XLA Modules:
  0.0 68.2 jit_solution(16532009278207556164)
XLA Ops:
  0.6 65.2 %substep.1 = (f32[27,4,32,256]{3,2,1,0:T(8,128)S(1)}, f32[4,4,27]{2,1,0:T(4,128)S(1)}) custom-call(f32[27,4,32,256]{3,2,1,0:T(8,128)} %tf.1, f32[3,4,32,256]{3,2,1,0:T(8,128)} %vel.1, s32[1,32]{1,0:T(1,128)} %bitcast.3, f32[8,5,32,128]{3,2,1,0:T(8,128)} %constant.12.clone.tab_hbm, bf16[2,3,512,256]{3,2,1,0:T(8,128)(2,1)} %constant.13.clone.fwd_hbm, ...), custom_call_target="tpu_custom_call" | custom-call | tf_op jit(solution)/shard_map/substep/pallas_call | solution.py:698
  65.8 1.8 %copy.13 = f32[27,4,32,256]{3,2,1,0:T(8,128)} copy(f32[27,4,32,256]{3,2,1,0:T(8,128)S(1)} %get-tuple-element.8) | data formatting | bytes 7077888
  67.6 0.6 copy.14

commit v4 on v3

--- a/solution.py
+++ b/solution.py
@@ -16,7 +16,7 @@
 STAGES = 9
 AHEAD = 3
 ELAG = 1
-PIECES = ((0, 1), (1, 4), (4, 9))
+PIECES = ((0, 1), (1, 3), (3, 5), (5, 7), (7, 9))
 ACROSS = 2
 LAG = 12
 BEHIND = 4
@@ -24,9 +24,11 @@
 HELP = 0
 FAR = 0
 VIA = 2
-PLAN = ("FH", "OF", "OH", "FH", "OF", "OH", "OF", "OH", "OH")
-FAR_WORK = (("L", 0), ("H", 0), ("H", 1), ("H", 3), ("H", 4), ("H", 6))
+PLAN = ("FH", "OF", "OH", "FH", "OF", "OH", "OH", "OO", "OH")
+FAR_WORK = (("L", 0), ("H", 0), ("H", 1), ("H", 3), ("H", 4))
 OWN = tuple(n for n in range(STAGES) if "O" in PLAN[n])
+DOUBLE = PLAN.index("OO")
+SECOND = STAGES
 HELPED = tuple(n for n in range(STAGES) if "H" in PLAN[n])
 FARRED = tuple(n for n in range(STAGES) if "F" in PLAN[n])
 LIGHT_FAR = tuple(n for kind, n in FAR_WORK if kind == "L")
@@ -441,6 +443,18 @@
                 def _(p=p):
                     a_copy(n, p, theta, octet, n, a_send).start()
 
+        @pl.when(heavy & (n == DOUBLE))
+        def _():
+            for p in workers:
+
+                @pl.when(p == phi)
+                def _(p=p):
+                    pltpu.make_async_copy(chunk(n, p, 2), rx.at[SECOND, phi], a_recv.at[SECOND]).start()
+
+                @pl.when(p != phi)
+                def _(p=p):
+                    a_copy(n, p, theta, 2, SECOND, a_send).start()
+
         @pl.when(light & member(n, LIGHT_FAR))
         def _():
             slot = pick(rank(n, LIGHT_FAR), [k for k, (kind, _) in enumerate(FAR_WORK) if kind == "L"])
@@ -474,9 +488,11 @@
             def _(k=k):
                 wait_theta(k)
 
-        @pl.when(n == 0)
-        def _():
-            send_theta(2)
+        for k in range(2, len(PIECES)):
+
+            @pl.when(n == PIECES[k][0] - 3)
+            def _(k=k):
+                send_theta(k)
 
         for m in range(3):
             i = main_i + m
@@ -509,13 +525,6 @@
         send(n, 1)
 
     half_rows = pl.ds(pl.multiple_of(my_half * 8, 8), 8)
-
-    def b_copy(n, p):
-        return pltpu.make_async_remote_copy(
-            src_ref=yb.at[n, p],
-            dst_ref=res.at[pl.ds(3 * n, 3), my_i, pl.ds(pl.multiple_of((octet + my_half) * 8, 8), 8), :],
-            send_sem=b_send, recv_sem=b_recv.at[n],
-            device_id={"phi": p}, device_id_type=MESH)
 
     def gather_copy(slot, p):
         return pltpu.make_async_remote_copy(
@@ -548,7 +557,7 @@
 
         on_light = far & (pick(slot, far_light) == 1)
         far_rows = jnp.where(on_light, light_octet, far_octet(pick(slot, far_stage)))
-        rows = jnp.where(far, far_rows, jnp.where(helper, 2, octet)) + my_half
+        rows = jnp.where(far, far_rows, jnp.where(helper | (slot == SECOND), 2, octet)) + my_half
         mine = pl.ds(pl.multiple_of(rows * 8, 8), 8)
         kept_rows = keep[jnp.where(on_light, 2, jnp.where(source, 0, 1)), mine, :]
         kept_rows = jnp.concatenate([kept_rows, kept_rows], axis=1)
@@ -562,11 +571,14 @@
 
         @pl.when(source)
         def _():
-            pltpu.make_async_copy(
-                yb.at[slot, phi], res.at[pl.ds(3 * slot, 3), my_i, mine, :], b_recv.at[slot]
-            ).start()
+            n = jnp.where(slot == SECOND, DOUBLE, slot)
+            here = res.at[pl.ds(3 * n, 3), my_i, mine, :]
+            pltpu.make_async_copy(yb.at[slot, phi], here, b_recv.at[n]).start()
             for k in range(1, PHI):
-                b_copy(slot, others(k)).start()
+                pltpu.make_async_remote_copy(
+                    src_ref=yb.at[slot, others(k)], dst_ref=here, send_sem=b_send, recv_sem=b_recv.at[n],
+                    device_id={"phi": others(k)}, device_id_type=MESH,
+                ).start()
 
         @pl.when(jnp.logical_not(source))
         def _():
@@ -623,9 +635,14 @@
 
         at = t - jnp.where(helper, HELP, jnp.where(far, FAR, jnp.where(light, LIGHT_BEHIND, BEHIND)))
 
-        @pl.when(busy(at - late))
-        def _():
-            work(at - late)
+        slot = at - late
+
+        def work_on(m, _):
+            work(jnp.where(m == 1, SECOND, slot))
+            return 0
+
+        halves = jnp.where(busy(slot), 1, 0) + jnp.where(heavy & (slot == DOUBLE), 1, 0)
+        lax.fori_loop(0, halves, work_on, 0)
 
         @pl.when((helper | far) & busy(at - ELAG - 1))
         def _():
@@ -669,8 +686,8 @@
             drain(rx.at[0, pl.ds(0, 2)], across_send.at[1, n])
             drain(vb.at[0, :, pl.ds(0, 3)], via_send.at[0, n])
             drain(vb.at[0, :, pl.ds(0, 1)], via_send.at[1, n])
-        drain(rx.at[pl.ds(0, len(OWN)), pl.ds(0, 7)], a_send)
-        drain(yb.at[pl.ds(0, len(OWN)), pl.ds(0, 7)], b_send)
+        drain(rx.at[pl.ds(0, len(OWN) + 1), pl.ds(0, 7)], a_send)
+        drain(yb.at[pl.ds(0, len(OWN) + 1), pl.ds(0, 7)], b_send)
 
     @pl.when(light)
     def _():
@@ -721,8 +738,8 @@
             pltpu.VMEM((3, 32, 128), F32),
             pltpu.VMEM((32, 128), F32),
             pltpu.VMEM((27, 4, 32, 256), F32),
-            pltpu.VMEM((STAGES, PHI, 3, 8, 256), F32),
-            pltpu.VMEM((STAGES, PHI, 3, 8, 256), F32),
+            pltpu.VMEM((STAGES + 1, PHI, 3, 8, 256), F32),
+            pltpu.VMEM((STAGES + 1, PHI, 3, 8, 256), F32),
             pltpu.VMEM((STAGES, 3, 4, 16, 256), F32),
             pltpu.VMEM((len(FARRED), 3, 4, 16, 256), F32),
             pltpu.VMEM((32, 128), F32),
@@ -739,7 +756,7 @@
             dma((2, ACROSS)),
             dma((2, len(FARRED))),
             dma,
-            dma((STAGES,)),
+            dma((STAGES + 1,)),
             dma,
             dma((STAGES,)),
             dma,

time: 68.8 us -> 64.2 us (0.933)
  Pallas kernels: 65.2 us -> 61 us
    pallas_call x1, Pallas kernels: 65.2 us -> 61 us  [body(): pl.pallas_call(kernel, out_shape=(jax.ShapeDtypeStruct((27, 4, 32, 256),...]
where the time goes in v4:
time: 64.2 us; the launch traced here: 64.1 us
  Pallas kernels  61 us (95%)
  local copies, waits for them, and re-layouts  2.39 us (4%)
    pallas_call x1, Pallas kernels, body(): pl.pallas_call(kernel, out_shape=(jax.ShapeDtypeStruct((27, 4, 32, 256),...  61 us
    unnamed x2, local copies, waits for them, and re-layouts  2.39 us

profile of v4, /device:TPU:1, one launch (start us, length us, event | category | flops | bytes accessed | tf_op | source)
XLA Modules:
  0.0 64.1 jit_solution(6132889424550786567)
XLA Ops:
  0.6 61.0 %substep.1 = (f32[27,4,32,256]{3,2,1,0:T(8,128)S(1)}, f32[4,4,27]{2,1,0:T(4,128)S(1)}) custom-call(f32[27,4,32,256]{3,2,1,0:T(8,128)} %tf.1, f32[3,4,32,256]{3,2,1,0:T(8,128)} %vel.1, s32[1,32]{1,0:T(1,128)} %bitcast.3, f32[8,5,32,128]{3,2,1,0:T(8,128)} %constant.12.clone.tab_hbm, bf16[2,3,512,256]{3,2,1,0:T(8,128)(2,1)} %constant.13.clone.fwd_hbm, ...), custom_call_target="tpu_custom_call" | custom-call | tf_op jit(solution)/shard_map/substep/pallas_call | solution.py:715
  61.7 1.8 %copy.13 = f32[27,4,32,256]{3,2,1,0:T(8,128)} copy(f32[27,4,32,256]{3,2,1,0:T(8,128)S(1)} %get-tuple-element.8) | data formatting | bytes 7077888
  63.5 0.6 copy.14

commit v5 on v4

--- a/solution.py
+++ b/solution.py
@@ -580,7 +580,19 @@
                     device_id={"phi": others(k)}, device_id_type=MESH,
                 ).start()
 
-        @pl.when(jnp.logical_not(source))
+        straight = helper & (slot == HELPED[-1])
+
+        @pl.when(straight)
+        def _():
+            for k in range(PHI):
+                p = others(k)
+                pltpu.make_async_remote_copy(
+                    src_ref=yb.at[slot, p], dst_ref=res.at[pl.ds(3 * HELPED[-1], 3), my_i, mine, :],
+                    send_sem=b_send, recv_sem=b_recv.at[HELPED[-1]],
+                    device_id={"theta": heavy_at, "phi": p}, device_id_type=MESH,
+                ).start()
+
+        @pl.when(jnp.logical_not(source | straight))
         def _():
             pltpu.make_async_copy(
                 yb.at[slot, phi], rel.at[slot, :, my_i, half_rows, :], rel_recv.at[slot]
@@ -644,9 +656,11 @@
         halves = jnp.where(busy(slot), 1, 0) + jnp.where(heavy & (slot == DOUBLE), 1, 0)
         lax.fori_loop(0, halves, work_on, 0)
 
-        @pl.when((helper | far) & busy(at - ELAG - 1))
-        def _():
-            relay(at - ELAG - 1)
+        last = at - ELAG - 1
+
+        @pl.when(((helper & (last != HELPED[-1])) | far) & busy(last))
+        def _():
+            relay(last)
 
         @pl.when(t >= LAG)
         def _():
@@ -698,8 +712,9 @@
 
     @pl.when(helper)
     def _():
-        drain(yb.at[pl.ds(0, len(HELPED)), pl.ds(0, 7)], b_send)
-        drain(rel.at[pl.ds(0, len(HELPED))], rel_send)
+        drain(yb.at[pl.ds(0, len(HELPED) - 1), pl.ds(0, 7)], b_send)
+        drain(yb.at[0], b_send)
+        drain(rel.at[pl.ds(0, len(HELPED) - 1)], rel_send)
 
     @pl.when(far)
     def _():

time: 64.2 us -> 64.7 us (level)
  no operation moved by 1% of the time
where the time goes in v5:
time: 64.7 us; the launch traced here: 64.6 us
  Pallas kernels  61.6 us (95%)
  local copies, waits for them, and re-layouts  2.39 us (4%)
    pallas_call x1, Pallas kernels, body(): pl.pallas_call(kernel, out_shape=(jax.ShapeDtypeStruct((27, 4, 32, 256),...  61.6 us
    unnamed x2, local copies, waits for them, and re-layouts  2.39 us

profile of v5, /device:TPU:1, one launch (start us, length us, event | category | flops | bytes accessed | tf_op | source)
XLA Modules:
  0.0 64.6 jit_solution(5919916906959021249)
XLA Ops:
  0.6 61.6 %substep.1 = (f32[27,4,32,256]{3,2,1,0:T(8,128)S(1)}, f32[4,4,27]{2,1,0:T(4,128)S(1)}) custom-call(f32[27,4,32,256]{3,2,1,0:T(8,128)} %tf.1, f32[3,4,32,256]{3,2,1,0:T(8,128)} %vel.1, s32[1,32]{1,0:T(1,128)} %bitcast.3, f32[8,5,32,128]{3,2,1,0:T(8,128)} %constant.12.clone.tab_hbm, bf16[2,3,512,256]{3,2,1,0:T(8,128)(2,1)} %constant.13.clone.fwd_hbm, ...), custom_call_target="tpu_custom_call" | custom-call | tf_op jit(solution)/shard_map/substep/pallas_call | solution.py:730
  62.2 1.8 %copy.13 = f32[27,4,32,256]{3,2,1,0:T(8,128)} copy(f32[27,4,32,256]{3,2,1,0:T(8,128)S(1)} %get-tuple-element.8) | data formatting | bytes 7077888
  64.0 0.6 copy.14
